TPU v7x, 256 devices: a whole 4x4x8 slice. The times are simulated.
256 devices in a mesh: node: 32 (over y_lo, z, core), local: 8 (over x, y_hi).
Axes of the slice: x: 4, y: 4 (y_hi: 2, y_lo: 2; y = y_hi * 2 + y_lo), z: 8, core: 2. Of those that a mesh axis runs over, the one named last changes fastest.
Arguments:
- acts: bfloat16 [32768, 4096], P(('node', 'local')), may hold values from -6 to 6
- grads_out: bfloat16 [32768, 8192], P(('node', 'local')), may hold values from -6 to 6
- base_output_weight: bfloat16 [4096, 8192], P('local', 'node'), may hold values from -0.09375 to 0.09375
- down_adapter_matrix: bfloat16 [16, 4096], replicated, may hold values from -0.09375 to 0.09375
- b_up: bfloat16 [16, 8192], replicated, may hold values from -0.0625 to 0.0625
Outputs:
- input_activation_gradient: bfloat16 [32768, 4096], P(('node', 'local'))
- grad_down: float32 [16, 4096], replicated
- grad_up: float32 [16, 8192], replicated
All inputs are finite; a program needn't handle non-finite values.
Results may differ from a plain program's by a relative error of at most 0.0034.
Values may be sent and summed in bfloat16 or wider, within the bound.
No kernel may reach another device: no remote copies, remote signals or barrier semaphores. Data moves between devices by JAX's collectives and lax.ppermute only.
A program may use at most 128 MiB of HBM per device.

v0:
```python
import math

import jax
import jax.numpy as jnp
from jax import lax
from jax.sharding import PartitionSpec as P


def reduce_adapter(grad_down, grad_up):
    return lax.psum((grad_down, grad_up), ("node", "local"))


def local(acts, grads_out, base_output_weight, down_adapter_matrix, b_up):
    tok_rows = acts.shape[0]
    total_tokens = tok_rows * lax.axis_size("node") * lax.axis_size("local")
    norm_factor = 2.0 / math.sqrt(total_tokens)
    low = jnp.einsum(
        "tk,rk->tr", acts, down_adapter_matrix, preferred_element_type=jnp.float32
    ).astype(jnp.bfloat16)
    backward_lowrank = jnp.einsum(
        "td,rd->tr", grads_out, b_up, preferred_element_type=jnp.float32
    ).astype(jnp.bfloat16)
    part_down = norm_factor * jnp.einsum(
        "tr,tk->rk", backward_lowrank, acts, preferred_element_type=jnp.float32
    )
    part_up = norm_factor * jnp.einsum(
        "tr,td->rd", low, grads_out, preferred_element_type=jnp.float32
    )
    lowrank_contribution = 2.0 * jnp.dot(
        backward_lowrank, down_adapter_matrix, preferred_element_type=jnp.float32
    )
    node_grads = lax.all_gather(grads_out, "local", axis=0, tiled=True)
    frozen_contribution = jnp.einsum(
        "td,kd->tk",
        node_grads,
        lax.all_gather(base_output_weight, "node", axis=1, tiled=True),
        preferred_element_type=jnp.float32,
    )
    backward_result = lax.all_to_all(
        frozen_contribution, "local", split_axis=0, concat_axis=1, tiled=True
    )
    input_activation_gradient = (backward_result + lowrank_contribution).astype(jnp.bfloat16)
    summed = reduce_adapter(part_down, part_up)
    return (input_activation_gradient, summed[0], summed[1])


def solution(mesh):
    in_specs = (
        P(("node", "local"), None),
        P(("node", "local"), None),
        P("local", "node"),
        P(),
        P(),
    )
    out_specs = (P(("node", "local"), None), P(), P())
    return jax.shard_map(local, mesh=mesh, in_specs=in_specs, out_specs=out_specs, check_vma=False)
```

profile of v0, /device:TPU:2, one launch (start us, length us, event | category | flops | bytes accessed | tf_op | source)
XLA Modules:
  0.0 591.0 jit_solution(1379784272407785680)
XLA Ops:
  8.0 0.0 copy-start
  8.0 0.0 all-gather.5.cloned.1.call-start
  8.1 0.7 all-gather.5.cloned.1.call-update
  8.7 0.0 all-gather.3.cloned.1.call-start
  8.8 0.7 all-gather.3.cloned.1.call-update
  9.5 93.7 %all-gather.5.cloned.1.call-done = bf16[512,8192]{1,0:T(8,128)(2,1)} async-done(((bf16[512,256]{1,0:T(8,128)(2,1)}), bf16[512,8192]{1,0:T(8,128)(2,1)}) %all-gather.5.cloned.1.call-update) | async-done | bytes 8388624 | tf_op jit(solution)/shard_map/all_gather | solution.py:36
  103.2 190.6 %all-gather.3.cloned.1.call-done = bf16[1024,8192]{1,0:T(8,128)(2,1)} async-done(((bf16[128,8192]{1,0:T(8,128)(2,1)}), bf16[1024,8192]{1,0:T(8,128)(2,1)}) %all-gather.3.cloned.1.call-update) | async-done | bytes 16777232 | tf_op jit(solution)/shard_map/all_gather | solution.py:32
  293.8 15.8 %fusion.2 = f32[1024,512]{1,0:T(8,128)} fusion(bf16[1024,8192]{1,0:T(8,128)(2,1)} %all-gather.3.cloned.1.call-done, bf16[512,8192]{1,0:T(8,128)(2,1)} %all-gather.5.cloned.1.call-done), kind=kOutput, calls=%fused_computation.7 | convolution fusion | flops 8589934592 | bytes 27262976 | tf_op jit(solution)/shard_map/td,kd->tk/dot_general | solution.py:33
  309.5 6.1 %all-to-all-start = ((f32[8,128,512]{2,1,0:T(8,128)}), f32[8,128,512]{2,1,0:T(8,128)}, u32[]{:S(2)}, u32[]{:S(2)}) async-start(f32[8,128,512]{2,1,0:T(8,128)} %bitcast.16), calls=%async_computation | async-start | bytes 4194304 | tf_op jit(solution)/shard_map/all_to_all | solution.py:39
  315.6 0.0 all-reduce.3.cloned.1.call-start
  315.6 0.0 copy-done.1
  315.6 0.0 copy-done.3
  315.6 0.6 convolution_convert_fusion.1
  316.3 0.0 copy-done
  316.3 1.0 convolution_multiply_fusion.2
  317.3 0.0 copy-done.2
  317.3 2.1 convolution_multiply_fusion
  319.4 0.0 all-reduce.3.cloned.1.call-update
  319.4 24.8 %all-to-all-done = f32[8,128,512]{2,1,0:T(8,128)} async-done(((f32[8,128,512]{2,1,0:T(8,128)}), f32[8,128,512]{2,1,0:T(8,128)}, u32[]{:S(2)}, u32[]{:S(2)}) %all-to-all-start) | async-done | bytes 2097184 | tf_op jit(solution)/shard_map/all_to_all | solution.py:39
  344.2 1.8 copy.9
  346.0 1.4 fusion.1
  347.4 232.6 %all-reduce.3.cloned.1.call-done = (f32[16,4096]{1,0:T(8,128)}, f32[16,8192]{1,0:T(8,128)}) async-done(((f32[16,4096]{1,0:T(8,128)}, f32[16,8192]{1,0:T(8,128)}), (f32[16,4096]{1,0:T(8,128)}, f32[16,8192]{1,0:T(8,128)})) %all-reduce.3.cloned.1.call-update) | async-done | bytes 786448 | tf_op jit(solution)/shard_map/psum | solution.py:10
  580.1 1.7 copy.12
  581.7 1.9 copy.13
  (3 shorter events, 0.0 us)
Async XLA Ops:
  8.0 308.3 %copy-start = (bf16[128,4096]{1,0:T(8,128)(2,1)S(1)}, bf16[128,4096]{1,0:T(8,128)(2,1)}, u32[]{:S(2)}) copy-start(bf16[128,4096]{1,0:T(8,128)(2,1)} %param.5) | copy-start | bytes 3145732
  8.0 95.2 %all-gather.5.cloned.1.call-start = ((), (), s32[]{:S(2)}) async-start(), calls=%async_computation.2 | async-start | bytes 8650752 | tf_op jit(solution)/shard_map/all_gather | solution.py:36
  8.7 285.0 %all-gather.3.cloned.1.call-start = ((), (), s32[]{:S(2)}) async-start(), calls=%async_computation.1 | async-start | bytes 18874368 | tf_op jit(solution)/shard_map/all_gather | solution.py:32
  309.5 6.1 %copy-start.1 = (bf16[128,8192]{1,0:T(8,128)(2,1)S(1)}, bf16[128,8192]{1,0:T(8,128)(2,1)}, u32[]{:S(2)}) copy-start(bf16[128,8192]{1,0:T(8,128)(2,1)} %param.6) | copy-start | bytes 6291460
  309.5 6.1 %copy-start.3 = (bf16[16,8192]{1,0:T(8,128)(2,1)S(1)}, bf16[16,8192]{1,0:T(8,128)(2,1)}, u32[]{:S(2)}) copy-start(bf16[16,8192]{1,0:T(8,128)(2,1)} %param.9) | copy-start | bytes 786436
  309.5 34.7 %all-to-all-start = ((f32[8,128,512]{2,1,0:T(8,128)}), f32[8,128,512]{2,1,0:T(8,128)}, u32[]{:S(2)}, u32[]{:S(2)}) async-start(f32[8,128,512]{2,1,0:T(8,128)} %bitcast.16), calls=%async_computation | async-start | bytes 4194304 | tf_op jit(solution)/shard_map/all_to_all | solution.py:39
  315.6 1.6 copy-start.2
  315.6 264.4 %all-reduce.3.cloned.1.call-start = ((), (), s32[]{:S(2)}) async-start(), calls=%async_computation.3 | async-start | bytes 1572864 | tf_op jit(solution)/shard_map/psum | solution.py:10
Sparse Core Ops, SparseCore 0:
  10.6 92.5 all-gather.4
  105.8 187.8 all-gather.2
Sparse Core Ops, SparseCore 1:
  322.4 257.7 all-reduce.2
where the time goes:
time: 591 us
  waiting for transfers between devices  543 us (92%)
  matrix products  21 us (4%)
  between operations  15.5 us (3%)
  starting transfers between devices  6.16 us (1%)
    psum x1, waiting for transfers between devices, reduce_adapter(): return lax.psum((grad_down, grad_up), ('node', 'local'))  233 us
    all_gather x1, waiting for transfers between devices, local(): node_grads = lax.all_gather(grads_out, 'local', axis=0, tiled=True)  191 us
    all_gather x1, waiting for transfers between devices, local(): lax.all_gather(base_output_weight, 'node', axis=1, tiled=True)  93.7 us
    all_to_all x1, waiting for transfers between devices, local(): lax.all_to_all(frozen_contribution, 'local', split_axis=0, concat_axis=1,...  24.8 us
    dot_general x1, matrix products, local(): jnp.einsum('td,kd->tk', node_grads, lax.all_gather(base_output_weight, 'n...  15.8 us
  transfers between devices with their start and end apart: 4, of which 4 were waited for; matrix products, arithmetic and copies ran while one was open for 1% of the time, Pallas kernels for 0%

commit v1 on v0

v1 whole, which is shorter than its diff:
```python
import math

import jax
import jax.numpy as jnp
from jax import lax
from jax.sharding import Mesh, PartitionSpec as P

Y = ("yhi", "ylo")
GROUP = ("yhi", "ylo", "core")
REST = ("x", "z")
TOKENS = ("ylo", "z", "core", "x", "yhi")


def gather_by_exchange(value, axes, n):
    return lax.all_to_all(jnp.broadcast_to(value[None], (n, *value.shape)), axes, 0, 0, tiled=True)


def reduce_adapter(part_down, part_up):
    rank = part_down.shape[0]
    both = jnp.concatenate([part_down, part_up], axis=1)
    width = both.shape[1]
    both = both.reshape(rank, 8, width // 8).transpose(1, 0, 2)
    mine = jnp.sum(lax.all_to_all(both, GROUP, 0, 0, tiled=True), axis=0)
    mine = mine.reshape(32, 1, rank * width // 256)
    mine = jnp.sum(lax.all_to_all(mine, REST, 0, 0, tiled=True), axis=0)
    mine = gather_by_exchange(mine, REST, 32).reshape(rank, width // 8)
    both = gather_by_exchange(mine, GROUP, 8)
    both = both.transpose(1, 0, 2).reshape(rank, width)
    return both[:, : part_down.shape[1]], both[:, part_down.shape[1] :]


def local(acts, grads_out, base_output_weight, down_adapter_matrix, b_up):
    rows, hd = acts.shape
    d = grads_out.shape[1]
    norm_factor = 2.0 / math.sqrt(rows * 256)
    w = lax.all_to_all(base_output_weight, "core", split_axis=0, concat_axis=1, tiled=True)
    w = lax.all_gather(w, REST, axis=0, tiled=False)
    w = w.reshape(4, 8, *w.shape[1:])
    halves = grads_out.reshape(rows, 2, d // 2).transpose(1, 0, 2)
    halves = jnp.broadcast_to(halves[None], (2, 2, rows, d // 2)).reshape(4, rows, d // 2)
    g = lax.all_to_all(halves, Y, 0, 0, tiled=True)

    low = jnp.einsum("tk,rk->tr", acts, down_adapter_matrix, preferred_element_type=jnp.float32).astype(jnp.bfloat16)
    back_low = jnp.einsum("td,rd->tr", grads_out, b_up, preferred_element_type=jnp.float32).astype(jnp.bfloat16)
    part_down = norm_factor * jnp.einsum("tr,tk->rk", back_low, acts, preferred_element_type=jnp.float32)
    part_up = norm_factor * jnp.einsum("tr,td->rd", low, grads_out, preferred_element_type=jnp.float32)
    grad_down, grad_up = reduce_adapter(part_down, part_up)
    lowrank = 2.0 * jnp.dot(back_low, down_adapter_matrix, preferred_element_type=jnp.float32)

    g = lax.all_gather(g, "core", axis=1, tiled=False)
    g = g.reshape(8 * rows, 8, d // 16)
    part = jnp.einsum("tzd,xzkd->txk", g, w, preferred_element_type=jnp.float32)
    part = part.astype(jnp.bfloat16).reshape(8, rows, hd // 4)
    part = lax.all_to_all(part, GROUP, 0, 0, tiled=True)
    part = part.reshape(2, 2, 2, rows, 4, hd // 16).astype(jnp.float32)
    frozen = (part[:, 0] + part[:, 1]).transpose(2, 3, 0, 1, 4).reshape(rows, hd)
    return (frozen + lowrank).astype(jnp.bfloat16), grad_down, grad_up


def solution(mesh):
    fine = Mesh(mesh.devices.reshape(2, 8, 2, 4, 2), ("ylo", "z", "core", "x", "yhi"))
    in_specs = (
        P(TOKENS, None),
        P(TOKENS, None),
        P(("x", "yhi"), ("ylo", "z", "core")),
        P(),
        P(),
    )
    out_specs = (P(TOKENS, None), P(), P())
    return jax.shard_map(local, mesh=fine, in_specs=in_specs, out_specs=out_specs, check_vma=False)
```

time: 591 us -> 263 us (0.45)
  waiting for transfers between devices: 543 us -> 73.4 us
  blocking collectives: 0 us -> 108 us
  local copies, waits for them, and re-layouts: 5.36 us -> 34.1 us
    all_gather x2, waiting for transfers between devices: 284 us -> 47.8 us  [the longest x1 47.8 us: local(): w = lax.all_gather(w, REST, axis=0, tiled=False)]
    psum x1 -> x0, waiting for transfers between devices: 233 us -> none  [reduce_adapter(): return lax.psum((grad_down, grad_up), ('node', 'local'))]
    all_to_all x0 -> x5, blocking collectives: none -> 108 us  [the longest x1 53.2 us: local(): g = lax.all_to_all(halves, Y, 0, 0, tiled=True)]
    unnamed x10 -> x12, local copies, waits for them, and re-layouts: 3.56 us -> 13.7 us
    reshape x0 -> x6, local copies, waits for them, and re-layouts: none -> 8.32 us  [the longest x1 3.38 us: local(): halves = grads_out.reshape(rows, 2, d // 2).transpose(1, 0, 2)]
    all_to_all x1 -> x2, waiting for transfers between devices: 24.8 us -> 25.6 us  [the longest x1 25.6 us: local(): part = lax.all_to_all(part, GROUP, 0, 0, tiled=True)]
  transfers between devices with their start and end apart: 4 -> 4, of which waited for: 4 -> 2; matrix products, arithmetic and copies ran while one was open for 1% -> 17% of each run, Pallas kernels for 0% -> 0%
where the time goes in v1:
time: 263 us; the launch traced here: 261 us
  blocking collectives  108 us (41%)
  waiting for transfers between devices  73.4 us (28%)
  local copies, waits for them, and re-layouts  34.1 us (13%)
  matrix products  20.8 us (8%)
  between operations  14.2 us (5%)
  starting transfers between devices  8.09 us (3%)
    all_to_all x1, blocking collectives, local(): g = lax.all_to_all(halves, Y, 0, 0, tiled=True)  53.2 us
    all_gather x1, waiting for transfers between devices, local(): w = lax.all_gather(w, REST, axis=0, tiled=False)  47.8 us
    all_to_all x1, waiting for transfers between devices, local(): part = lax.all_to_all(part, GROUP, 0, 0, tiled=True)  25.6 us
    all_to_all x1, blocking collectives, reduce_adapter(): mine = jnp.sum(lax.all_to_all(mine, REST, 0, 0, tiled=True), axis=0)  20.5 us
    all_to_all x1, blocking collectives, reduce_adapter(): mine = jnp.sum(lax.all_to_all(both, GROUP, 0, 0, tiled=True), axis=0)  15.7 us
    dot_general x1, matrix products, local(): part = jnp.einsum('tzd,xzkd->txk', g, w, preferred_element_type=jnp.float32)  15.4 us
    all_to_all x1, blocking collectives, gather_by_exchange(): lax.all_to_all(jnp.broadcast_to(value[None], (n, *value.shape)), axes, 0,...  14.1 us
    unnamed x12, local copies, waits for them, and re-layouts  13.7 us
  transfers between devices with their start and end apart: 4, of which 2 were waited for; matrix products, arithmetic and copies ran while one was open for 17% of the time, Pallas kernels for 0%

profile of v1, /device:TPU:2, one launch (start us, length us, event | category | flops | bytes accessed | tf_op | source)
XLA Modules:
  0.0 260.8 jit_solution(11758764836912257623)
XLA Ops:
  7.2 3.4 %reshape.48 = bf16[128,2,4096]{2,1,0:T(2,128)(2,1)S(1)} reshape(bf16[128,8192]{1,0:T(8,128)(2,1)} %param.6) | data formatting | bytes 4194304 | tf_op jit(solution)/shard_map/reshape | solution.py:39
  10.6 1.3 copy.38
  12.5 53.2 %all_to_all.46 = bf16[4,128,4096]{2,1,0:T(8,128)(2,1)} all-to-all(bf16[4,128,4096]{2,1,0:T(8,128)(2,1)S(1)} %bitcast.49), channel_id=1, replica_groups=mesh['ylo'=2,'z'=8,'core'=2,'x'=4,'yhi'=2] {'yhi','ylo'}, dimensions={0} | all-to-all | bytes 8388608 | tf_op jit(solution)/shard_map/all_to_all | solution.py:41
  65.7 0.9 copy-done.4
  66.6 4.6 %all_to_all.47 = bf16[2,256,256]{2,1,0:T(8,128)(2,1)} all-to-all(bf16[2,256,256]{2,1,0:T(8,128)(2,1)S(1)} %bitcast.62), channel_id=1, replica_groups=mesh['ylo'=2,'z'=8,'core'=2,'x'=4,'yhi'=2] {'core'}, dimensions={0} | all-to-all | bytes 524288 | tf_op jit(solution)/shard_map/all_to_all | solution.py:36
  71.2 1.1 copy.39
  73.2 1.6 convolution_convert_fusion.1
  75.1 2.1 convolution_multiply_fusion
  77.2 1.2 pad_maximum_fusion
  78.4 15.7 %all_to_all.48 = f32[8,16,1536]{2,1,0:T(8,128)S(1)} all-to-all(f32[8,16,1536]{2,1,0:T(8,128)S(1)} %bitcast.60), channel_id=1, replica_groups=mesh['ylo'=2,'z'=8,'core'=2,'x'=4,'yhi'=2] {'yhi','ylo','core'}, dimensions={0} | all-to-all | bytes 1572864 | tf_op jit(solution)/shard_map/all_to_all | solution.py:23
  94.3 20.5 %all_to_all.49 = f32[32,1,768]{2,1,0:T(1,128)S(1)} all-to-all(f32[32,1,768]{2,1,0:T(1,128)S(1)} %reshape.55), channel_id=1, replica_groups=mesh['ylo'=2,'z'=8,'core'=2,'x'=4,'yhi'=2] {'x','z'}, dimensions={0} | all-to-all | bytes 196608 | tf_op jit(solution)/shard_map/all_to_all | solution.py:25
  114.9 14.1 %all_to_all.50 = f32[32,1,768]{2,1,0:T(1,128)S(1)} all-to-all(f32[32,1,768]{2,1,0:T(1,128)S(1)} %broadcast_in_dim.9), channel_id=1, replica_groups=mesh['ylo'=2,'z'=8,'core'=2,'x'=4,'yhi'=2] {'x','z'}, dimensions={0} | all-to-all | bytes 196608 | tf_op jit(solution)/shard_map/all_to_all | solution.py:15
  129.2 1.0 broadcast_in_dim.22
  130.2 3.7 %all-to-all-start.6 = ((f32[8,16,1536]{2,1,0:T(8,128)}), f32[8,16,1536]{2,1,0:T(8,128)S(1)}, u32[]{:S(2)}, u32[]{:S(2)}) async-start(f32[8,16,1536]{2,1,0:T(8,128)} %broadcast_in_dim.22), calls=%async_computation.6 | async-start | bytes 1572864 | tf_op jit(solution)/shard_map/all_to_all | solution.py:15
  133.9 12.2 %copy.50 = bf16[128,8,8,512]{3,2,1,0:T(8,128)(2,1)} copy(bf16[128,8,8,512]{3,1,2,0:T(8,128)(2,1)} %bitcast.51) | data formatting | bytes 16777216
  146.1 47.8 %all-gather.4.cloned.1.call-done = bf16[32,256,512]{2,1,0:T(8,128)(2,1)} async-done(((bf16[1,256,512]{2,1,0:T(8,128)(2,1)}), bf16[32,256,512]{2,1,0:T(8,128)(2,1)}) %all-gather.4.cloned.1.call-update) | async-done | bytes 8388624 | tf_op jit(solution)/shard_map/all_gather | solution.py:37
  193.9 15.4 %bitcast_convert_fusion = bf16[1024,4,256]{2,0,1:T(8,128)(2,1)} fusion(bf16[4,8,256,512]{3,2,1,0:T(8,128)(2,1)} %bitcast.63, bf16[1024,8,512]{2,1,0:T(8,128)(2,1)} %bitcast.52), kind=kOutput, calls=%fused_computation.8 | convolution fusion | flops 8590983168 | bytes 18874368 | tf_op jit(solution)/shard_map/tzd,xzkd->txk/dot_general | solution.py:52
  209.3 3.2 %copy.42 = bf16[1024,4,256]{0,2,1:T(8,128)(2,1)S(1)} copy(bf16[1024,4,256]{2,0,1:T(8,128)(2,1)} %bitcast_convert_fusion) | data formatting | bytes 4194304 | tf_op jit(solution)/shard_map/convert_element_type | solution.py:53
  213.1 1.7 copy.43
  214.8 4.3 %all-to-all-start.2 = ((bf16[8,128,1024]{1,2,0:T(8,128)(2,1)}), bf16[8,128,1024]{1,2,0:T(8,128)(2,1)S(1)}, u32[]{:S(2)}, u32[]{:S(2)}) async-start(bf16[8,128,1024]{1,2,0:T(8,128)(2,1)} %copy.43), calls=%async_computation.2 | async-start | bytes 4194304 | tf_op jit(solution)/shard_map/all_to_all | solution.py:54
  220.7 25.6 %all-to-all-done.2 = bf16[8,128,1024]{1,2,0:T(8,128)(2,1)S(1)} async-done(((bf16[8,128,1024]{1,2,0:T(8,128)(2,1)}), bf16[8,128,1024]{1,2,0:T(8,128)(2,1)S(1)}, u32[]{:S(2)}, u32[]{:S(2)}) %all-to-all-start.2) | async-done | bytes 2097184 | tf_op jit(solution)/shard_map/all_to_all | solution.py:54
  247.0 2.5 copy.44
  249.5 3.0 %reshape.53 = f32[128,4096]{1,0:T(8,128)S(1)} reshape(f32[128,4,2,2,256]{4,3,2,1,0:T(2,128)} %copy.44) | data formatting | bytes 4194304 | tf_op jit(solution)/shard_map/reshape | solution.py:56
  252.5 1.4 fusion.4
  (31 shorter events, 5.3 us)
Async XLA Ops:
  7.2 67.7 %copy-start = (bf16[128,4096]{1,0:T(8,128)(2,1)S(1)}, bf16[128,4096]{1,0:T(8,128)(2,1)}, u32[]{:S(2)}) copy-start(bf16[128,4096]{1,0:T(8,128)(2,1)} %param.5) | copy-start | bytes 3145732
  7.2 126.8 %all-gather.6.cloned.1.call-start = ((), (), s32[]{:S(2)}) async-start(), calls=%async_computation.8 | async-start | bytes 12582912 | tf_op jit(solution)/shard_map/all_gather | solution.py:50
  65.6 1.0 copy-start.4
  65.6 7.6 %copy-start.2 = (bf16[128,8192]{1,0:T(8,128)(2,1)S(1)}, bf16[128,8192]{1,0:T(8,128)(2,1)}, u32[]{:S(2)}) copy-start(bf16[128,8192]{1,0:T(8,128)(2,1)} %param.6) | copy-start | bytes 6291460
  65.7 128.2 %all-gather.4.cloned.1.call-start = ((), (), s32[]{:S(2)}) async-start(), calls=%async_computation.7 | async-start | bytes 8650752 | tf_op jit(solution)/shard_map/all_gather | solution.py:37
  73.2 1.9 copy-start.3
  130.2 84.6 %all-to-all-start.6 = ((f32[8,16,1536]{2,1,0:T(8,128)}), f32[8,16,1536]{2,1,0:T(8,128)S(1)}, u32[]{:S(2)}, u32[]{:S(2)}) async-start(f32[8,16,1536]{2,1,0:T(8,128)} %broadcast_in_dim.22), calls=%async_computation.6 | async-start | bytes 1572864 | tf_op jit(solution)/shard_map/all_to_all | solution.py:15
  214.8 31.5 %all-to-all-start.2 = ((bf16[8,128,1024]{1,2,0:T(8,128)(2,1)}), bf16[8,128,1024]{1,2,0:T(8,128)(2,1)S(1)}, u32[]{:S(2)}, u32[]{:S(2)}) async-start(bf16[8,128,1024]{1,2,0:T(8,128)(2,1)} %copy.43), calls=%async_computation.2 | async-start | bytes 4194304 | tf_op jit(solution)/shard_map/all_to_all | solution.py:54
  249.5 4.5 %copy-start.1 = (bf16[128,4096]{1,0:T(8,128)(2,1)S(1)}, bf16[128,4096]{1,0:T(8,128)(2,1)}, u32[]{:S(2)}) copy-start(bf16[128,4096]{1,0:T(8,128)(2,1)} %param.5) | copy-start | bytes 3145732
Sparse Core Ops, SparseCore 0:
  65.8 26.1 all-gather.5
  95.1 98.7 all-gather.3

commit v2 on v1

v2 whole, which is shorter than its diff:
```python
import functools
import math

import jax
import jax.numpy as jnp
from jax import lax
from jax.experimental import pallas as pl
from jax.experimental.pallas import tpu as pltpu
from jax.sharding import Mesh, PartitionSpec as P

GROUP = ("yhi", "ylo", "core")
REST = ("x", "z")
TOKENS = ("ylo", "z", "core", "x", "yhi")
HOPS = {4: (0, 1, 3, 2)}
F32 = jnp.float32


def place_of(y):
    return 2 * (y % 2) + y // 2


def gather_by_exchange(value, axes, n):
    return lax.all_to_all(jnp.broadcast_to(value[None], (n, *value.shape)), axes, 0, 0, tiled=True)


def swap_cores(value):
    return lax.ppermute(value, "core", [(0, 1), (1, 0)])


def scatter_adapter(part_down, part_up):
    rank = part_down.shape[0]
    both = jnp.concatenate([part_down, part_up], axis=1)
    width = both.shape[1]
    both = both.reshape(rank, 8, width // 8).transpose(1, 0, 2)
    mine = jnp.sum(lax.all_to_all(both, GROUP, 0, 0, tiled=True), axis=0)
    return lax.all_to_all(mine.reshape(32, 1, rank * width // 256), REST, 0, 0, tiled=True)


def gather_adapter(terms, rank, split):
    width = terms.size * 8 // rank
    mine = gather_by_exchange(jnp.sum(terms, axis=0), REST, 32).reshape(rank, width // 8)
    both = gather_by_exchange(mine, GROUP, 8)
    both = both.transpose(1, 0, 2).reshape(rank, width)
    return both[:, :split], both[:, split:]


def product_kernel(place, *refs):
    blocks, (w, out, a_all, w_all, a_sem, w_sem) = refs[:8], refs[8:]
    rows = blocks[0].shape[0]
    kc, depth = w.shape[-2:]

    def w_copies(x):
        return [
            pltpu.make_async_copy(w.at[x, z], w_all.at[pl.ds(x * kc, kc), pl.ds(z * depth, depth)], w_sem.at[8 * x + z])
            for z in range(8)
        ]

    def a_copies(i):
        for j, half in ((i, place[4]), (4 + i, place[5])):
            at = pl.multiple_of((2 * i + half) * rows, rows)
            yield pltpu.make_async_copy(blocks[j], a_all.at[pl.ds(at, rows)], a_sem.at[j])

    for copies in (w_copies(0), w_copies(1), a_copies(0), a_copies(1), a_copies(2), a_copies(3), w_copies(2), w_copies(3)):
        for copy in copies:
            copy.start()
    for side in range(2):
        for copy in w_copies(2 * side) + w_copies(2 * side + 1):
            copy.wait()
        columns = slice(2 * side * kc, 2 * side * kc + 2 * kc)

        @pl.loop(0, 2)
        def _(m):
            if side == 0:

                @pl.loop(0, 2)
                def _(i):
                    for j in (2 * m + i, 4 + 2 * m + i):
                        pltpu.make_async_copy(blocks[0], a_all.at[pl.ds(0, rows)], a_sem.at[j]).wait()

            a = a_all[pl.ds(pl.multiple_of(m * 4 * rows, 4 * rows), 4 * rows)]
            part = lax.dot_general(a, w_all[columns], (((1,), (1,)), ((), ())), preferred_element_type=F32)
            part = part.astype(jnp.bfloat16)
            for i in range(2):
                owner = place[2 * m + i]
                out[2 * owner, :, columns] = part[2 * i * rows : (2 * i + 1) * rows]
                out[2 * owner + 1, :, columns] = part[(2 * i + 1) * rows : (2 * i + 2) * rows]


def product(place, blocks, w):
    rows, k = blocks[0].shape
    kc = w.shape[-2]
    return pl.pallas_call(
        product_kernel,
        out_shape=jax.ShapeDtypeStruct((8, rows, 4 * kc), jnp.bfloat16),
        in_specs=[pl.BlockSpec(memory_space=pltpu.SMEM)] + [pl.BlockSpec(memory_space=pl.ANY)] * 9,
        out_specs=pl.BlockSpec(memory_space=pltpu.VMEM),
        scratch_shapes=[
            pltpu.VMEM((8 * rows, k), jnp.bfloat16),
            pltpu.VMEM((4 * kc, k), jnp.bfloat16),
            pltpu.SemaphoreType.DMA((8,)),
            pltpu.SemaphoreType.DMA((32,)),
        ],
        compiler_params=pltpu.CompilerParams(vmem_limit_bytes=48 * 2**20),
        cost_estimate=pl.CostEstimate(
            flops=64 * rows * kc * k, bytes_accessed=2 * (8 * rows * k + 4 * kc * k + 32 * rows * kc), transcendentals=0
        ),
    )(place, *blocks, w)


def finish_kernel(*refs):
    parts, back_low, down, out = refs[:-3], *refs[-3:]
    back = back_low[...]
    for yhi in range(2):
        for core in range(2):
            one, two = 4 * yhi + core, 4 * yhi + 2 + core
            sums = [p[one].astype(F32) + p[two].astype(F32) for p in parts]
            for x in range(4):
                cols = pl.ds(x * 1024 + yhi * 512 + core * 256, 256)
                frozen = [s[:, x * (s.shape[1] // 4) : (x + 1) * (s.shape[1] // 4)] for s in sums]
                frozen = jnp.concatenate(frozen, axis=1) if len(frozen) > 1 else frozen[0]
                lowrank = 2.0 * jnp.dot(back, down[:, cols], preferred_element_type=F32)
                out[:, cols] = (frozen + lowrank).astype(out.dtype)


def finish(parts, back_low, down):
    rows, rank = back_low.shape
    hd = down.shape[1]
    step = rows // 4
    return pl.pallas_call(
        finish_kernel,
        grid=(4,),
        out_shape=jax.ShapeDtypeStruct((rows, hd), jnp.bfloat16),
        in_specs=[pl.BlockSpec((8, step, p.shape[2]), lambda i: (0, i, 0)) for p in parts]
        + [pl.BlockSpec((step, rank), lambda i: (i, 0)), pl.BlockSpec((rank, hd), lambda i: (0, 0))],
        out_specs=pl.BlockSpec((step, hd), lambda i: (i, 0)),
        compiler_params=pltpu.CompilerParams(vmem_limit_bytes=32 * 2**20),
        cost_estimate=pl.CostEstimate(flops=2 * rows * rank * hd, bytes_accessed=6 * rows * hd, transcendentals=0),
    )(*parts, back_low, down)


def local(acts, grads_out, base_output_weight, down_adapter_matrix, b_up):
    rows, hd = acts.shape
    d = grads_out.shape[1]
    norm_factor = 2.0 / math.sqrt(rows * 256)
    ylo, core = lax.axis_index("ylo"), lax.axis_index("core")
    y = 2 * lax.axis_index("yhi") + ylo
    half = base_output_weight.shape[0] // 2
    mine = lax.dynamic_slice_in_dim(base_output_weight, core * half, half, 0)
    other = swap_cores(lax.dynamic_slice_in_dim(base_output_weight, (1 - core) * half, half, 0))
    w = jnp.where(core == 0, jnp.concatenate([mine, other], axis=1), jnp.concatenate([other, mine], axis=1))
    w = lax.all_gather(w, REST, axis=0, tiled=False).reshape(4, 8, *w.shape)
    keep = lax.dynamic_slice_in_dim(grads_out, ylo * (d // 2), d // 2, 1)
    give = lax.dynamic_slice_in_dim(grads_out, (1 - ylo) * (d // 2), d // 2, 1)
    blocks = [keep]
    for hop, value in zip(HOPS[4][1:], (give, give, keep)):
        blocks.append(lax.ppermute(value, ("ylo", "yhi"), [(place_of(i), place_of((i + hop) % 4)) for i in range(4)]))
    blocks += [swap_cores(b) for b in blocks]
    from_y = (y - jnp.array(HOPS[4])) % 4
    place = jnp.concatenate([from_y, jnp.stack([core, 1 - core])]).astype(jnp.int32)

    low = jnp.einsum("tk,rk->tr", acts, down_adapter_matrix, preferred_element_type=F32).astype(jnp.bfloat16)
    back_low = jnp.einsum("td,rd->tr", grads_out, b_up, preferred_element_type=F32).astype(jnp.bfloat16)
    part_down = norm_factor * jnp.einsum("tr,tk->rk", back_low, acts, preferred_element_type=F32)
    part_up = norm_factor * jnp.einsum("tr,td->rd", low, grads_out, preferred_element_type=F32)
    terms = scatter_adapter(part_down, part_up)

    parts = [product(place, blocks, w)]
    parts = [lax.all_to_all(p, GROUP, 0, 0, tiled=True) for p in parts]
    grad_down, grad_up = gather_adapter(terms, low.shape[1], hd)
    return finish(parts, back_low, down_adapter_matrix), grad_down, grad_up


def solution(mesh):
    fine = Mesh(mesh.devices.reshape(2, 8, 2, 4, 2), ("ylo", "z", "core", "x", "yhi"))
    in_specs = (
        P(TOKENS, None),
        P(TOKENS, None),
        P(("x", "yhi"), ("ylo", "z", "core")),
        P(),
        P(),
    )
    out_specs = (P(TOKENS, None), P(), P())
    return jax.shard_map(local, mesh=fine, in_specs=in_specs, out_specs=out_specs, check_vma=False)
```

time: 263 us -> 175 us (0.67)
  blocking collectives: 108 us -> 0 us
  starting transfers between devices: 8.09 us -> 34.7 us
  local copies, waits for them, and re-layouts: 34.1 us -> 11 us
  Pallas kernels: 0 us -> 17.9 us
  matrix products: 20.8 us -> 3.85 us
  waiting for transfers between devices: 73.4 us -> 89.5 us
    all_to_all x5 -> x0, blocking collectives: 108 us -> none  [the longest x1 53.2 us: local(): g = lax.all_to_all(halves, Y, 0, 0, tiled=True)]
    all_gather x2 -> x1, waiting for transfers between devices: 47.8 us -> 0.49 us  [local(): w = lax.all_gather(w, REST, axis=0, tiled=False).reshape(4, 8, *w.shape)]
    ppermute x0 -> x8, waiting for transfers between devices: none -> 38.5 us  [the longest x3 37.2 us: local(): lax.ppermute(value, ('ylo', 'yhi'), [(place_of(i), place_of((i + hop) % 4...]
    pallas_call x0 -> x2, Pallas kernels: none -> 17.9 us  [the longest x1 15.7 us: product(): pl.pallas_call(product_kernel, out_shape=jax.ShapeDtypeStruct((8, rows, 4...]
    dot_general x5 -> x3, matrix products: 20.8 us -> 3.85 us  [the longest x1 2.89 us: local(): jnp.einsum('tr,td->rd', low, grads_out, preferred_element_type=F32)]
    all_to_all x1 -> x3, waiting for transfers between devices: 25.6 us -> 41 us  [the longest x1 24.5 us: local(): parts = [lax.all_to_all(p, GROUP, 0, 0, tiled=True) for p in parts]]
    all_to_all x1 -> x3, starting transfers between devices: 4.28 us -> 19.5 us  [the longest x1 11.6 us: scatter_adapter(): lax.all_to_all(mine.reshape(32, 1, rank * width // 256), REST, 0, 0, tile...]
    unnamed x12, local copies, waits for them, and re-layouts: 13.7 us -> 0.91 us
  transfers between devices with their start and end apart: 4 -> 14, of which waited for: 2 -> 7; matrix products, arithmetic and copies ran while one was open for 17% -> 8% of each run, Pallas kernels for 0% -> 9%
where the time goes in v2:
time: 175 us; the launch traced here: 173 us
  waiting for transfers between devices  89.5 us (51%)
  starting transfers between devices  34.7 us (20%)
  Pallas kernels  17.9 us (10%)
  between operations  14.3 us (8%)
  local copies, waits for them, and re-layouts  11 us (6%)
  matrix products  3.85 us (2%)
    ppermute x3, waiting for transfers between devices, local(): lax.ppermute(value, ('ylo', 'yhi'), [(place_of(i), place_of((i + hop) % 4...  37.2 us
    all_to_all x1, waiting for transfers between devices, local(): parts = [lax.all_to_all(p, GROUP, 0, 0, tiled=True) for p in parts]  24.5 us
    pallas_call x1, Pallas kernels, product(): pl.pallas_call(product_kernel, out_shape=jax.ShapeDtypeStruct((8, rows, 4...  15.7 us
    all_to_all x1, starting transfers between devices, scatter_adapter(): lax.all_to_all(mine.reshape(32, 1, rank * width // 256), REST, 0, 0, tile...  11.6 us
    all_to_all x1, waiting for transfers between devices, scatter_adapter(): lax.all_to_all(mine.reshape(32, 1, rank * width // 256), REST, 0, 0, tile...  9.66 us
    all_to_all x2, waiting for transfers between devices, gather_by_exchange(): lax.all_to_all(jnp.broadcast_to(value[None], (n, *value.shape)), axes, 0,...  9.52 us
    all_to_all x2, starting transfers between devices, gather_by_exchange(): lax.all_to_all(jnp.broadcast_to(value[None], (n, *value.shape)), axes, 0,...  8.85 us
    all_to_all x1, waiting for transfers between devices, scatter_adapter(): mine = jnp.sum(lax.all_to_all(both, GROUP, 0, 0, tiled=True), axis=0)  6.87 us
  transfers between devices with their start and end apart: 14, of which 7 were waited for; matrix products, arithmetic and copies ran while one was open for 8% of the time, Pallas kernels for 9%

profile of v2, /device:TPU:2, one launch (start us, length us, event | category | flops | bytes accessed | tf_op | source)
XLA Modules:
  0.0 172.5 jit_solution(14988725564978087392)
XLA Ops:
  7.2 1.1 dynamic-slice_bitcast_fusion
  8.4 1.3 collective-permute-done.7
  10.6 2.8 %constant_dynamic-slice_fusion.1 = (bf16[128,4096]{1,0:T(8,128)(2,1)}, bf16[128,4096]{1,0:T(8,128)(2,1)S(1)}) fusion(bf16[128,8192]{1,0:T(8,128)(2,1)} %param.7, s32[]{:T(128)S(6)} %select_n.36, s32[]{:T(128)S(6)} %select_n.35), kind=kLoop, calls=%fused_computation.12 | loop fusion | bytes 4194312 | tf_op jit(solution)/shard_map/dynamic_slice | solution.py:153
  13.5 1.6 collective-permute-start
  15.0 1.7 collective-permute-start.1
  16.7 2.0 %collective-permute-start.2 = (bf16[128,4096]{1,0:T(8,128)(2,1)S(1)}, bf16[128,4096]{1,0:T(8,128)(2,1)}, u32[]{:S(2)}, u32[]{:S(2)}) collective-permute-start(bf16[128,4096]{1,0:T(8,128)(2,1)S(1)} %get-tuple-element.4.refs_0_), channel_id=1, source_target_pairs={{0,1},{128,129},{1,0},{129,128},{2,3},{130,131},{3,2},{131,130},{4... | collective-permute-start | bytes 3145736 | tf_op jit(solution)/shard_map/ppermute | solution.py:156
  19.7 2.9 %convolution_multiply_fusion = f32[16,8192]{1,0:T(8,128)S(1)} fusion(bf16[128,8192]{1,0:T(8,128)(2,1)} %param.7, bf16[128,4096]{1,0:T(8,128)(2,1)S(1)} %copy-done, bf16[16,4096]{1,0:T(8,128)(2,1)S(1)} %copy-done.1), kind=kOutput, calls=%fused_computation | convolution fusion | flops 50464768 | bytes 3801088 | tf_op jit(solution)/shard_map/tr,td->rd/dot_general | solution.py:164
  22.6 1.0 copy.19
  23.7 3.6 %all-to-all-start.1 = ((f32[8,16,1536]{2,1,0:T(8,128)}), f32[8,16,1536]{2,1,0:T(8,128)S(1)}, u32[]{:S(2)}, u32[]{:S(2)}) async-start(f32[8,16,1536]{2,1,0:T(8,128)} %bitcast.24), calls=%async_computation.1 | async-start | bytes 1572864 | tf_op jit(solution)/shard_map/all_to_all | solution.py:35
  27.6 37.2 %collective-permute-done.2.refs_3_ = bf16[128,4096]{1,0:T(8,128)(2,1)} collective-permute-done((bf16[128,4096]{1,0:T(8,128)(2,1)S(1)}, bf16[128,4096]{1,0:T(8,128)(2,1)}, u32[]{:S(2)}, u32[]{:S(2)}) %collective-permute-start.2) | collective-permute-done | bytes 1048608 | tf_op jit(solution)/shard_map/ppermute | solution.py:156
  65.4 6.9 %all-to-all-done.1 = f32[8,16,1536]{2,1,0:T(8,128)S(1)} async-done(((f32[8,16,1536]{2,1,0:T(8,128)}), f32[8,16,1536]{2,1,0:T(8,128)S(1)}, u32[]{:S(2)}, u32[]{:S(2)}) %all-to-all-start.1) | async-done | bytes 786464 | tf_op jit(solution)/shard_map/all_to_all | solution.py:35
  73.1 11.6 %all-to-all-start.2 = ((f32[32,1,768]{2,1,0:T(1,128)}), f32[32,1,768]{2,1,0:T(1,128)S(1)}, u32[]{:S(2)}, u32[]{:S(2)}) async-start(f32[32,1,768]{2,1,0:T(1,128)} %reshape.81), calls=%async_computation.2 | async-start | bytes 196608 | tf_op jit(solution)/shard_map/all_to_all | solution.py:36
  84.7 9.7 %all-to-all-done.2 = f32[32,1,768]{2,1,0:T(1,128)S(1)} async-done(((f32[32,1,768]{2,1,0:T(1,128)}), f32[32,1,768]{2,1,0:T(1,128)S(1)}, u32[]{:S(2)}, u32[]{:S(2)}) %all-to-all-start.2) | async-done | bytes 98336 | tf_op jit(solution)/shard_map/all_to_all | solution.py:36
  95.2 5.1 %all-to-all-start.3 = ((f32[32,1,768]{2,1,0:T(1,128)}), f32[32,1,768]{2,1,0:T(1,128)S(1)}, u32[]{:S(2)}, u32[]{:S(2)}) async-start(f32[32,1,768]{2,1,0:T(1,128)} %broadcast_in_dim.6), calls=%async_computation.3 | async-start | bytes 196608 | tf_op jit(solution)/shard_map/all_to_all | solution.py:23
  100.4 9.5 %all-to-all-done.3 = f32[32,1,768]{2,1,0:T(1,128)S(1)} async-done(((f32[32,1,768]{2,1,0:T(1,128)}), f32[32,1,768]{2,1,0:T(1,128)S(1)}, u32[]{:S(2)}, u32[]{:S(2)}) %all-to-all-start.3) | async-done | bytes 98336 | tf_op jit(solution)/shard_map/all_to_all | solution.py:23
  110.2 1.0 broadcast_in_dim.15
  111.1 3.7 %all-to-all-start.4 = ((f32[8,16,1536]{2,1,0:T(8,128)}), f32[8,16,1536]{2,1,0:T(8,128)S(1)}, u32[]{:S(2)}, u32[]{:S(2)}) async-start(f32[8,16,1536]{2,1,0:T(8,128)} %broadcast_in_dim.15), calls=%async_computation.4 | async-start | bytes 1572864 | tf_op jit(solution)/shard_map/all_to_all | solution.py:23
  115.4 15.7 %shard_map.85 = bf16[8,128,1024]{2,1,0:T(8,128)(2,1)} custom-call(s32[6]{0:T(128)S(1)} %pad_add_fusion.place, bf16[128,4096]{1,0:T(8,128)(2,1)S(1)} %get-tuple-element.4.refs_0_, bf16[128,4096]{1,0:T(8,128)(2,1)} %collective-permute-done.refs_1_, bf16[128,4096]{1,0:T(8,128)(2,1)} %collective-permute-done.1.refs_2_, ...), custom_call_target="tpu_custom_call" | custom-call | flops 8589934592 | bytes 18874368 | tf_op jit(solution)/shard_map/pallas_call | solution.py:92
  131.2 0.9 copy-done.3
  132.0 4.3 %all-to-all-start = ((bf16[8,128,1024]{2,1,0:T(8,128)(2,1)}), bf16[8,128,1024]{2,1,0:T(8,128)(2,1)S(1)}, u32[]{:S(2)}, u32[]{:S(2)}) async-start(bf16[8,128,1024]{2,1,0:T(8,128)(2,1)} %shard_map.85), calls=%async_computation | async-start | bytes 4194304 | tf_op jit(solution)/shard_map/all_to_all | solution.py:168
  136.3 1.2 copy.17
  137.5 0.8 slice.9
  139.1 24.5 %all-to-all-done.refs_0_ = bf16[8,128,1024]{2,1,0:T(8,128)(2,1)S(1)} async-done(((bf16[8,128,1024]{2,1,0:T(8,128)(2,1)}), bf16[8,128,1024]{2,1,0:T(8,128)(2,1)S(1)}, u32[]{:S(2)}, u32[]{:S(2)}) %all-to-all-start) | async-done | bytes 2097184 | tf_op jit(solution)/shard_map/all_to_all | solution.py:168
  163.5 2.2 %shard_map.86 = bf16[128,4096]{1,0:T(8,128)(2,1)} custom-call(bf16[8,128,1024]{2,1,0:T(8,128)(2,1)S(1)} %all-to-all-done.refs_0_, bf16[128,16]{1,0:T(8,128)(2,1)S(1)} %convolution_convert_fusion.refs_1_, bf16[16,4096]{1,0:T(8,128)(2,1)S(1)} %copy-done.1), custom_call_target="tpu_custom_call" | custom-call | flops 16777216 | bytes 3145728 | tf_op jit(solution)/shard_map/pallas_call | solution.py:129
  (39 shorter events, 6.2 us)
Async XLA Ops:
  7.2 12.2 %copy-start = (bf16[128,4096]{1,0:T(8,128)(2,1)S(1)}, bf16[128,4096]{1,0:T(8,128)(2,1)}, u32[]{:S(2)}) copy-start(bf16[128,4096]{1,0:T(8,128)(2,1)} %param.6) | copy-start | bytes 3145732
  7.2 108.2 %all-gather.2.cloned.1.call-start = ((), (), s32[]{:S(2)}) async-start(), calls=%async_computation.5 | async-start | bytes 8650752 | tf_op jit(solution)/shard_map/all_gather | solution.py:151
  8.3 1.4 collective-permute-start.7
  10.6 8.1 %copy-start.2 = (bf16[128,8192]{1,0:T(8,128)(2,1)S(1)}, bf16[128,8192]{1,0:T(8,128)(2,1)}, u32[]{:S(2)}) copy-start(bf16[128,8192]{1,0:T(8,128)(2,1)} %param.7) | copy-start | bytes 6291460
  10.6 8.1 %copy-start.4 = (bf16[16,8192]{1,0:T(8,128)(2,1)S(1)}, bf16[16,8192]{1,0:T(8,128)(2,1)}, u32[]{:S(2)}) copy-start(bf16[16,8192]{1,0:T(8,128)(2,1)} %param.10) | copy-start | bytes 786436
  13.5 6.2 %copy-start.1 = (bf16[16,4096]{1,0:T(8,128)(2,1)S(1)}, bf16[16,4096]{1,0:T(8,128)(2,1)}, u32[]{:S(2)}) copy-start(bf16[16,4096]{1,0:T(8,128)(2,1)} %refs_2_.1) | copy-start | bytes 393220
  13.5 51.3 %collective-permute-start = (bf16[128,4096]{1,0:T(8,128)(2,1)}, bf16[128,4096]{1,0:T(8,128)(2,1)}, u32[]{:S(2)}, u32[]{:S(2)}) collective-permute-start(bf16[128,4096]{1,0:T(8,128)(2,1)} %get-tuple-element.3), channel_id=1, source_target_pairs={{0,128},{128,1},{1,129},{129,0},{2,130},{130,3},{3,131},{131,2},{4... | collective-permute-start | bytes 3145736 | tf_op jit(solution)/shard_map/ppermute | solution.py:156
  15.0 50.3 %collective-permute-start.1 = (bf16[128,4096]{1,0:T(8,128)(2,1)}, bf16[128,4096]{1,0:T(8,128)(2,1)}, u32[]{:S(2)}, u32[]{:S(2)}) collective-permute-start(bf16[128,4096]{1,0:T(8,128)(2,1)} %get-tuple-element.3), channel_id=1, source_target_pairs={{0,129},{128,0},{1,128},{129,1},{2,131},{130,2},{3,130},{131,3},{4... | collective-permute-start | bytes 3145736 | tf_op jit(solution)/shard_map/ppermute | solution.py:156
  16.7 48.1 %collective-permute-start.2 = (bf16[128,4096]{1,0:T(8,128)(2,1)S(1)}, bf16[128,4096]{1,0:T(8,128)(2,1)}, u32[]{:S(2)}, u32[]{:S(2)}) collective-permute-start(bf16[128,4096]{1,0:T(8,128)(2,1)S(1)} %get-tuple-element.4.refs_0_), channel_id=1, source_target_pairs={{0,1},{128,129},{1,0},{129,128},{2,3},{130,131},{3,2},{131,130},{4... | collective-permute-start | bytes 3145736 | tf_op jit(solution)/shard_map/ppermute | solution.py:156
  22.6 77.7 %copy-start.5 = (s32[4]{0:T(128)S(1)}, s32[4]{0:T(128)}, u32[]{:S(2)}) copy-start(s32[4]{0:T(128)} %constant.50) | copy-start | bytes 52
  23.7 48.6 %all-to-all-start.1 = ((f32[8,16,1536]{2,1,0:T(8,128)}), f32[8,16,1536]{2,1,0:T(8,128)S(1)}, u32[]{:S(2)}, u32[]{:S(2)}) async-start(f32[8,16,1536]{2,1,0:T(8,128)} %bitcast.24), calls=%async_computation.1 | async-start | bytes 1572864 | tf_op jit(solution)/shard_map/all_to_all | solution.py:35
  27.2 87.7 %collective-permute-start.3 = (bf16[128,4096]{1,0:T(8,128)(2,1)S(1)}, bf16[128,4096]{1,0:T(8,128)(2,1)}, u32[]{:S(2)}, u32[]{:S(2)}) collective-permute-start(bf16[128,4096]{1,0:T(8,128)(2,1)S(1)} %get-tuple-element.4.refs_0_), channel_id=1, source_target_pairs={{0,8},{8,0},{1,9},{9,1},{2,10},{10,2},{3,11},{11,3},{4,12},{12,4},... | collective-permute-start | bytes 3145736 | tf_op jit(solution)/shard_map/ppermute | solution.py:27
  64.8 50.1 %collective-permute-start.6 = (bf16[128,4096]{1,0:T(8,128)(2,1)}, bf16[128,4096]{1,0:T(8,128)(2,1)}, u32[]{:S(2)}, u32[]{:S(2)}) collective-permute-start(bf16[128,4096]{1,0:T(8,128)(2,1)} %collective-permute-done.2.refs_3_), channel_id=1, source_target_pairs={{0,8},{8,0},{1,9},{9,1},{2,10},{10,2},{3,11},{11,3},{4,12},{12,4},... | collective-permute-start | bytes 3145736 | tf_op jit(solution)/shard_map/ppermute | solution.py:27
  64.8 50.1 %collective-permute-start.4 = (bf16[128,4096]{1,0:T(8,128)(2,1)}, bf16[128,4096]{1,0:T(8,128)(2,1)}, u32[]{:S(2)}, u32[]{:S(2)}) collective-permute-start(bf16[128,4096]{1,0:T(8,128)(2,1)} %collective-permute-done.refs_1_), channel_id=1, source_target_pairs={{0,8},{8,0},{1,9},{9,1},{2,10},{10,2},{3,11},{11,3},{4,12},{12,4},... | collective-permute-start | bytes 3145736 | tf_op jit(solution)/shard_map/ppermute | solution.py:27
  65.3 49.6 %collective-permute-start.5 = (bf16[128,4096]{1,0:T(8,128)(2,1)}, bf16[128,4096]{1,0:T(8,128)(2,1)}, u32[]{:S(2)}, u32[]{:S(2)}) collective-permute-start(bf16[128,4096]{1,0:T(8,128)(2,1)} %collective-permute-done.1.refs_2_), channel_id=1, source_target_pairs={{0,8},{8,0},{1,9},{9,1},{2,10},{10,2},{3,11},{11,3},{4,12},{12,4},... | collective-permute-start | bytes 3145736 | tf_op jit(solution)/shard_map/ppermute | solution.py:27
  73.1 21.3 %all-to-all-start.2 = ((f32[32,1,768]{2,1,0:T(1,128)}), f32[32,1,768]{2,1,0:T(1,128)S(1)}, u32[]{:S(2)}, u32[]{:S(2)}) async-start(f32[32,1,768]{2,1,0:T(1,128)} %reshape.81), calls=%async_computation.2 | async-start | bytes 196608 | tf_op jit(solution)/shard_map/all_to_all | solution.py:36
  95.2 14.8 %all-to-all-start.3 = ((f32[32,1,768]{2,1,0:T(1,128)}), f32[32,1,768]{2,1,0:T(1,128)S(1)}, u32[]{:S(2)}, u32[]{:S(2)}) async-start(f32[32,1,768]{2,1,0:T(1,128)} %broadcast_in_dim.6), calls=%async_computation.3 | async-start | bytes 196608 | tf_op jit(solution)/shard_map/all_to_all | solution.py:23
  111.1 20.0 %all-to-all-start.4 = ((f32[8,16,1536]{2,1,0:T(8,128)}), f32[8,16,1536]{2,1,0:T(8,128)S(1)}, u32[]{:S(2)}, u32[]{:S(2)}) async-start(f32[8,16,1536]{2,1,0:T(8,128)} %broadcast_in_dim.15), calls=%async_computation.4 | async-start | bytes 1572864 | tf_op jit(solution)/shard_map/all_to_all | solution.py:23
  131.1 0.9 copy-start.3
  132.0 31.5 %all-to-all-start = ((bf16[8,128,1024]{2,1,0:T(8,128)(2,1)}), bf16[8,128,1024]{2,1,0:T(8,128)(2,1)S(1)}, u32[]{:S(2)}, u32[]{:S(2)}) async-start(bf16[8,128,1024]{2,1,0:T(8,128)(2,1)} %shard_map.85), calls=%async_computation | async-start | bytes 4194304 | tf_op jit(solution)/shard_map/all_to_all | solution.py:168
Sparse Core Ops, SparseCore 0:
  11.2 104.1 all-gather.1

commit v3 on v1

v3 whole, which is shorter than its diff:
```python
import functools
import math

import jax
import jax.numpy as jnp
from jax import lax
from jax.experimental import pallas as pl
from jax.experimental.pallas import tpu as pltpu
from jax.sharding import Mesh, PartitionSpec as P

Y = ("yhi", "ylo")
GROUP = ("yhi", "ylo", "core")
REST = ("x", "z")
TOKENS = ("ylo", "z", "core", "x", "yhi")
HOPS = (0, 1, 3, 2)
F32 = jnp.float32


def place_of(y):
    return 2 * (y % 2) + y // 2


def gather_by_exchange(value, axes, n):
    return lax.all_to_all(jnp.broadcast_to(value[None], (n, *value.shape)), axes, 0, 0, tiled=True)


def along_y(value, hop):
    return lax.ppermute(value, ("ylo", "yhi"), [(place_of(i), place_of((i + hop) % 4)) for i in range(4)])


def scatter_group(part_down, part_up):
    rank = part_down.shape[0]
    both = jnp.concatenate([part_down, part_up], axis=1)
    width = both.shape[1]
    both = both.reshape(rank, 8, width // 8).transpose(1, 0, 2)
    return jnp.sum(lax.all_to_all(both, GROUP, 0, 0, tiled=True), axis=0)


def scatter_rest(mine):
    return lax.all_to_all(mine.reshape(32, 1, mine.size // 32), REST, 0, 0, tiled=True)


def gather_adapter(terms, rank, split):
    width = terms.size * 8 // rank
    mine = gather_by_exchange(jnp.sum(terms, axis=0), REST, 32).reshape(rank, width // 8)
    both = gather_by_exchange(mine, GROUP, 8)
    both = both.transpose(1, 0, 2).reshape(rank, width)
    return both[:, :split], both[:, split:]


def product_kernel(owner, *refs):
    blocks, (w, out, a_all, w_all, total, a_sem, w_sem) = refs[:4], refs[4:]
    rows, k = blocks[0].shape
    parts, _, kc, depth = w.shape
    wide = depth // 2

    def copies(i):
        yield pltpu.make_async_copy(w.at[i], w_all.at[i], w_sem.at[i])
        for j, block in enumerate(blocks):
            for ylo in range(2):
                source = block.at[:, pl.ds(pl.multiple_of(ylo * (k // 2) + i * wide, wide), wide)]
                target = a_all.at[i, pl.ds(j * rows, rows), pl.ds(ylo * wide, wide)]
                yield pltpu.make_async_copy(source, target, a_sem.at[i, 2 * j + ylo])

    @pl.loop(0, parts)
    def _(i):
        for copy in copies(i):
            copy.start()

    def terms(step):
        for q in range(2):
            for copy in copies(2 * step + q):
                copy.wait()
        return sum(
            lax.dot_general(
                a_all[2 * step + q],
                w_all[2 * step + q].reshape(4 * kc, depth),
                (((1,), (1,)), ((), ())),
                preferred_element_type=F32,
            )
            for q in range(2)
        )

    total[...] = terms(0)

    @pl.loop(1, parts // 2)
    def _(step):
        total[...] += terms(step)

    for j in range(4):
        out[owner[j]] = total[j * rows : (j + 1) * rows].astype(out.dtype)


def product(owner, blocks, w):
    rows, k = blocks[0].shape
    parts, _, kc, depth = w.shape
    return pl.pallas_call(
        product_kernel,
        out_shape=jax.ShapeDtypeStruct((4, rows, 4 * kc), jnp.bfloat16),
        in_specs=[pl.BlockSpec(memory_space=pltpu.SMEM)] + [pl.BlockSpec(memory_space=pl.ANY)] * 5,
        out_specs=pl.BlockSpec(memory_space=pltpu.VMEM),
        scratch_shapes=[
            pltpu.VMEM((parts, 4 * rows, depth), jnp.bfloat16),
            pltpu.VMEM((parts, 4, kc, depth), jnp.bfloat16),
            pltpu.VMEM((4 * rows, 4 * kc), F32),
            pltpu.SemaphoreType.DMA((parts, 8)),
            pltpu.SemaphoreType.DMA((parts,)),
        ],
        compiler_params=pltpu.CompilerParams(vmem_limit_bytes=48 * 2**20),
        cost_estimate=pl.CostEstimate(
            flops=32 * rows * kc * k, bytes_accessed=2 * (4 * rows * k + 4 * kc * k + 16 * rows * kc), transcendentals=0
        ),
    )(owner, *blocks, w)


def finish_kernel(parts, back_low, down, out):
    kc = parts.shape[2] // 4
    lowrank = 2.0 * jnp.dot(back_low[...], down[...], preferred_element_type=F32)
    for x in range(4):
        for y in range(4):
            columns = slice((4 * x + y) * kc, (4 * x + y + 1) * kc)
            frozen = parts[y, :, x * kc : (x + 1) * kc].astype(F32)
            out[:, columns] = (frozen + lowrank[:, columns]).astype(out.dtype)


def finish(parts, back_low, down):
    rows, rank = back_low.shape
    hd = down.shape[1]
    step = rows // 4
    return pl.pallas_call(
        finish_kernel,
        grid=(4,),
        out_shape=jax.ShapeDtypeStruct((rows, hd), jnp.bfloat16),
        in_specs=[
            pl.BlockSpec((4, step, hd // 4), lambda i: (0, i, 0)),
            pl.BlockSpec((step, rank), lambda i: (i, 0)),
            pl.BlockSpec((rank, hd), lambda i: (0, 0)),
        ],
        out_specs=pl.BlockSpec((step, hd), lambda i: (i, 0)),
        compiler_params=pltpu.CompilerParams(vmem_limit_bytes=32 * 2**20),
        cost_estimate=pl.CostEstimate(flops=2 * rows * rank * hd, bytes_accessed=4 * rows * hd, transcendentals=0),
    )(parts, back_low, down)


def local(acts, grads_out, base_output_weight, down_adapter_matrix, b_up):
    rows, hd = acts.shape
    d = grads_out.shape[1]
    norm_factor = 2.0 / math.sqrt(rows * 256)
    ylo = lax.axis_index("ylo")
    y = 2 * lax.axis_index("yhi") + ylo
    half = base_output_weight.shape[0] // 2
    mine = lax.dynamic_slice_in_dim(base_output_weight, ylo * half, half, 0)
    other = lax.dynamic_slice_in_dim(base_output_weight, (1 - ylo) * half, half, 0)
    other = lax.ppermute(other, "ylo", [(0, 1), (1, 0)])
    w = jnp.where(ylo == 0, jnp.concatenate([mine, other], axis=1), jnp.concatenate([other, mine], axis=1))
    w = lax.all_gather(w, ("z", "core", "x"), axis=0, tiled=False).reshape(16, 4, *w.shape)
    near = [along_y(grads_out, hop) for hop in HOPS[1:3]]

    low = jnp.einsum("tk,rk->tr", acts, down_adapter_matrix, preferred_element_type=F32).astype(jnp.bfloat16)
    back_low = jnp.einsum("td,rd->tr", grads_out, b_up, preferred_element_type=F32).astype(jnp.bfloat16)
    part_down = norm_factor * jnp.einsum("tr,tk->rk", back_low, acts, preferred_element_type=F32)
    part_up = norm_factor * jnp.einsum("tr,td->rd", low, grads_out, preferred_element_type=F32)
    total = scatter_group(part_down, part_up)
    total, far, *near = lax.optimization_barrier((total, grads_out, *near))
    blocks = [grads_out, *near, along_y(far, HOPS[3])]
    terms = scatter_rest(total)

    parts = product(((y - jnp.array(HOPS)) % 4).astype(jnp.int32), blocks, w)
    parts = lax.all_to_all(parts, Y, 0, 0, tiled=True)
    grad_down, grad_up = gather_adapter(terms, low.shape[1], hd)
    return finish(parts, back_low, down_adapter_matrix), grad_down, grad_up


def solution(mesh):
    fine = Mesh(mesh.devices.reshape(2, 8, 2, 4, 2), ("ylo", "z", "core", "x", "yhi"))
    in_specs = (
        P(TOKENS, None),
        P(TOKENS, None),
        P(("x", "yhi"), ("ylo", "z", "core")),
        P(),
        P(),
    )
    out_specs = (P(TOKENS, None), P(), P())
    return jax.shard_map(local, mesh=fine, in_specs=in_specs, out_specs=out_specs, check_vma=False)
```

time: 263 us -> 169 us (0.64)
  blocking collectives: 108 us -> 48.6 us
  waiting for transfers between devices: 73.4 us -> 39.3 us
  local copies, waits for them, and re-layouts: 34.1 us -> 8.02 us
  starting transfers between devices: 8.09 us -> 30.6 us
  Pallas kernels: 0 us -> 17.1 us
  matrix products: 20.8 us -> 4.68 us
    all_to_all x5 -> x1, blocking collectives: 108 us -> 48.6 us  [scatter_group(): return jnp.sum(lax.all_to_all(both, GROUP, 0, 0, tiled=True), axis=0)]
    all_gather x2 -> x1, waiting for transfers between devices: 47.8 us -> 0.01 us  [local(): lax.all_gather(w, ('z', 'core', 'x'), axis=0, tiled=False)]
    pallas_call x0 -> x2, Pallas kernels: none -> 17.1 us  [the longest x1 15 us: product(): pl.pallas_call(product_kernel, out_shape=jax.ShapeDtypeStruct((4, rows, 4...]
    dot_general x5 -> x3, matrix products: 20.8 us -> 4.68 us  [the longest x1 2.3 us: local(): jnp.einsum('td,rd->tr', grads_out, b_up, preferred_element_type=F32)]
    unnamed x12 -> x10, local copies, waits for them, and re-layouts: 13.7 us -> 0.99 us
    all_to_all x1 -> x2, starting transfers between devices: 4.28 us -> 15.1 us  [the longest x1 11.6 us: scatter_rest(): lax.all_to_all(mine.reshape(32, 1, mine.size // 32), REST, 0, 0, tiled=True)]
    all_to_all x1 -> x2, waiting for transfers between devices: 0.01 us -> 9.59 us  [gather_by_exchange(): lax.all_to_all(jnp.broadcast_to(value[None], (n, *value.shape)), axes, 0,...]
    ppermute x0 -> x4, waiting for transfers between devices: none -> 8.39 us  [the longest x3 4.41 us: along_y(): lax.ppermute(value, ('ylo', 'yhi'), [(place_of(i), place_of((i + hop) % 4...]
  transfers between devices with their start and end apart: 4 -> 9, of which waited for: 2 -> 5; matrix products, arithmetic and copies ran while one was open for 17% -> 8% of each run, Pallas kernels for 0% -> 9%
where the time goes in v3:
time: 169 us; the launch traced here: 167 us
  blocking collectives  48.6 us (29%)
  waiting for transfers between devices  39.3 us (23%)
  starting transfers between devices  30.6 us (18%)
  Pallas kernels  17.1 us (10%)
  between operations  14.2 us (8%)
  local copies, waits for them, and re-layouts  8.02 us (5%)
  matrix products  4.68 us (3%)
  other arithmetic  4.37 us (3%)
    all_to_all x1, blocking collectives, scatter_group(): return jnp.sum(lax.all_to_all(both, GROUP, 0, 0, tiled=True), axis=0)  48.6 us
    pallas_call x1, Pallas kernels, product(): pl.pallas_call(product_kernel, out_shape=jax.ShapeDtypeStruct((4, rows, 4...  15 us
    all_to_all x1, starting transfers between devices, scatter_rest(): lax.all_to_all(mine.reshape(32, 1, mine.size // 32), REST, 0, 0, tiled=True)  11.6 us
    all_to_all x1, waiting for transfers between devices, local(): parts = lax.all_to_all(parts, Y, 0, 0, tiled=True)  11.6 us
    all_to_all x1, waiting for transfers between devices, scatter_rest(): lax.all_to_all(mine.reshape(32, 1, mine.size // 32), REST, 0, 0, tiled=True)  9.71 us
    all_to_all x2, waiting for transfers between devices, gather_by_exchange(): lax.all_to_all(jnp.broadcast_to(value[None], (n, *value.shape)), axes, 0,...  9.59 us
    all_to_all x2, starting transfers between devices, gather_by_exchange(): lax.all_to_all(jnp.broadcast_to(value[None], (n, *value.shape)), axes, 0,...  9.4 us
    ppermute x3, starting transfers between devices, along_y(): lax.ppermute(value, ('ylo', 'yhi'), [(place_of(i), place_of((i + hop) % 4...  4.44 us
  transfers between devices with their start and end apart: 9, of which 5 were waited for; matrix products, arithmetic and copies ran while one was open for 8% of the time, Pallas kernels for 9%

profile of v3, /device:TPU:2, one launch (start us, length us, event | category | flops | bytes accessed | tf_op | source)
XLA Modules:
  0.0 166.8 jit_solution(17838035301270487466)
XLA Ops:
  7.3 1.8 %dynamic-slice_bitcast_fusion = (bf16[1,256,256]{2,1,0:T(8,128)(2,1)S(1)}, bf16[256,256]{1,0:T(8,128)(2,1)}) fusion(bf16[512,256]{1,0:T(8,128)(2,1)} %param.8, s32[]{:T(128)S(6)} %select_n.30, s32[]{:T(128)S(6)} %select_n.31), kind=kLoop, calls=%fused_computation.7 | loop fusion | bytes 524296 | tf_op jit(solution)/shard_map/concatenate | solution.py:155
  9.1 1.6 collective-permute-start.3
  10.6 4.0 %collective-permute-done.3 = bf16[256,256]{1,0:T(8,128)(2,1)} collective-permute-done((bf16[256,256]{1,0:T(8,128)(2,1)}, bf16[256,256]{1,0:T(8,128)(2,1)}, u32[]{:S(2)}, u32[]{:S(2)}) %collective-permute-start.3) | collective-permute-done | bytes 131104 | tf_op jit(solution)/shard_map/ppermute | solution.py:154
  14.6 1.8 %maximum_select_fusion = bf16[1,256,512]{2,1,0:T(8,128)(2,1)} fusion(bf16[1,256,256]{2,1,0:T(8,128)(2,1)} %bitcast.2, bf16[1,256,256]{2,1,0:T(8,128)(2,1)S(1)} %get-tuple-element.11, pred[]{:T(512)S(6)} %eq.5), kind=kLoop, calls=%fused_computation.6 | loop fusion | flops 1179648 | bytes 524289 | tf_op jit(solution)/shard_map/jit(_where)/select_n | solution.py:155
  16.4 1.7 collective-permute-start
  18.0 1.7 collective-permute-start.1
  19.7 2.3 %convolution_convert_fusion.back_low = bf16[128,16]{1,0:T(8,128)(2,1)S(1)} fusion(bf16[128,8192]{1,0:T(8,128)(2,1)} %refs_0_.1, bf16[16,8192]{1,0:T(8,128)(2,1)} %param.10), kind=kOutput, calls=%fused_computation.2 | convolution fusion | flops 33556480 | bytes 2363392 | tf_op jit(solution)/shard_map/td,rd->tr/dot_general | solution.py:160
  22.0 2.1 %convolution_multiply_fusion = f32[16,8192]{1,0:T(8,128)} fusion(bf16[128,8192]{1,0:T(8,128)(2,1)S(1)} %copy-done.1, bf16[128,4096]{1,0:T(8,128)(2,1)S(1)} %copy-done, bf16[16,4096]{1,0:T(8,128)(2,1)S(1)} %copy-done.3), kind=kOutput, calls=%fused_computation | convolution fusion | flops 50464768 | bytes 3801088 | tf_op jit(solution)/shard_map/tr,td->rd/dot_general | solution.py:162
  24.4 1.1 pad_maximum_fusion
  25.6 48.6 %all_to_all.25 = f32[8,16,1536]{2,1,0:T(8,128)} all-to-all(f32[8,16,1536]{2,1,0:T(8,128)S(1)} %bitcast.24), channel_id=1, replica_groups=mesh['ylo'=2,'z'=8,'core'=2,'x'=4,'yhi'=2] {'yhi','ylo','core'}, dimensions={0} | all-to-all | bytes 1572864 | tf_op jit(solution)/shard_map/all_to_all | solution.py:36
  74.2 1.2 reduce_sum.18
  75.4 1.1 collective-permute-start.2
  77.2 11.6 %all-to-all-start.2 = ((f32[32,1,768]{2,1,0:T(1,128)}), f32[32,1,768]{2,1,0:T(1,128)S(1)}, u32[]{:S(2)}, u32[]{:S(2)}) async-start(f32[32,1,768]{2,1,0:T(1,128)} %reshape.81), calls=%async_computation.2 | async-start | bytes 196608 | tf_op jit(solution)/shard_map/all_to_all | solution.py:40
  88.9 9.7 %all-to-all-done.2 = f32[32,1,768]{2,1,0:T(1,128)S(1)} async-done(((f32[32,1,768]{2,1,0:T(1,128)}), f32[32,1,768]{2,1,0:T(1,128)S(1)}, u32[]{:S(2)}, u32[]{:S(2)}) %all-to-all-start.2) | async-done | bytes 98336 | tf_op jit(solution)/shard_map/all_to_all | solution.py:40
  99.4 5.2 %all-to-all-start.3 = ((f32[32,1,768]{2,1,0:T(1,128)}), f32[32,1,768]{2,1,0:T(1,128)S(1)}, u32[]{:S(2)}, u32[]{:S(2)}) async-start(f32[32,1,768]{2,1,0:T(1,128)} %broadcast_in_dim.6), calls=%async_computation.3 | async-start | bytes 196608 | tf_op jit(solution)/shard_map/all_to_all | solution.py:24
  104.6 9.6 %all-to-all-done.3 = f32[32,1,768]{2,1,0:T(1,128)S(1)} async-done(((f32[32,1,768]{2,1,0:T(1,128)}), f32[32,1,768]{2,1,0:T(1,128)S(1)}, u32[]{:S(2)}, u32[]{:S(2)}) %all-to-all-start.3) | async-done | bytes 98336 | tf_op jit(solution)/shard_map/all_to_all | solution.py:24
  114.4 1.0 broadcast_in_dim.15
  115.4 4.2 %all-to-all-start.4 = ((f32[8,16,1536]{2,1,0:T(8,128)}), f32[8,16,1536]{2,1,0:T(8,128)}, u32[]{:S(2)}, u32[]{:S(2)}) async-start(f32[8,16,1536]{2,1,0:T(8,128)} %broadcast_in_dim.15), calls=%async_computation.4 | async-start | bytes 1572864 | tf_op jit(solution)/shard_map/all_to_all | solution.py:24
  119.7 4.4 %collective-permute-done.2.refs_3_ = bf16[128,8192]{1,0:T(8,128)(2,1)} collective-permute-done((bf16[128,8192]{1,0:T(8,128)(2,1)S(1)}, bf16[128,8192]{1,0:T(8,128)(2,1)}, u32[]{:S(2)}, u32[]{:S(2)}) %collective-permute-start.2) | collective-permute-done | bytes 2097184 | tf_op jit(solution)/shard_map/ppermute | solution.py:28
  124.1 15.0 %shard_map.85 = bf16[4,128,1024]{2,1,0:T(8,128)(2,1)S(1)} custom-call(s32[4]{0:T(128)S(1)} %and_select_fusion.owner, bf16[128,8192]{1,0:T(8,128)(2,1)S(1)} %copy-done.1, bf16[128,8192]{1,0:T(8,128)(2,1)} %collective-permute-done.refs_1_, bf16[128,8192]{1,0:T(8,128)(2,1)} %collective-permute-done.1.refs_2_, bf16[128,8192]{1,0:T(8,128)(2,1)} %collective-permute-done.2.refs_3_, ...), custom_call_target="tpu_custom_call" | custom-call | flops 8589934592 | bytes 26214400 | tf_op jit(solution)/shard_map/pallas_call | solution.py:97
  140.0 3.5 %all-to-all-start.1 = ((bf16[4,128,1024]{2,1,0:T(8,128)(2,1)}), bf16[4,128,1024]{2,1,0:T(8,128)(2,1)S(1)}, u32[]{:S(2)}, u32[]{:S(2)}) async-start(bf16[4,128,1024]{2,1,0:T(8,128)(2,1)} %copy-done.2), calls=%async_computation.1 | async-start | bytes 2097152 | tf_op jit(solution)/shard_map/all_to_all | solution.py:169
  143.5 1.2 copy.17
  146.3 11.6 %all-to-all-done.1.parts = bf16[4,128,1024]{2,1,0:T(8,128)(2,1)S(1)} async-done(((bf16[4,128,1024]{2,1,0:T(8,128)(2,1)}), bf16[4,128,1024]{2,1,0:T(8,128)(2,1)S(1)}, u32[]{:S(2)}, u32[]{:S(2)}) %all-to-all-start.1) | async-done | bytes 1048608 | tf_op jit(solution)/shard_map/all_to_all | solution.py:169
  157.9 2.1 %shard_map.86 = bf16[128,4096]{1,0:T(8,128)(2,1)} custom-call(bf16[4,128,1024]{2,1,0:T(8,128)(2,1)S(1)} %all-to-all-done.1.parts, bf16[128,16]{1,0:T(8,128)(2,1)S(1)} %convolution_convert_fusion.back_low, bf16[16,4096]{1,0:T(8,128)(2,1)S(1)} %copy-done.3), custom_call_target="tpu_custom_call" | custom-call | flops 16777216 | bytes 2097152 | tf_op jit(solution)/shard_map/pallas_call | solution.py:130
  (26 shorter events, 4.8 us)
Async XLA Ops:
  7.2 14.8 %copy-start = (bf16[128,4096]{1,0:T(8,128)(2,1)S(1)}, bf16[128,4096]{1,0:T(8,128)(2,1)}, u32[]{:S(2)}) copy-start(bf16[128,4096]{1,0:T(8,128)(2,1)} %param.6) | copy-start | bytes 3145732
  7.2 14.8 %copy-start.1 = (bf16[128,8192]{1,0:T(8,128)(2,1)S(1)}, bf16[128,8192]{1,0:T(8,128)(2,1)}, u32[]{:S(2)}) copy-start(bf16[128,8192]{1,0:T(8,128)(2,1)} %refs_0_.1) | copy-start | bytes 6291460
  7.2 14.8 %copy-start.3 = (bf16[16,4096]{1,0:T(8,128)(2,1)S(1)}, bf16[16,4096]{1,0:T(8,128)(2,1)}, u32[]{:S(2)}) copy-start(bf16[16,4096]{1,0:T(8,128)(2,1)} %down.1) | copy-start | bytes 393220
  7.2 116.9 %all-gather.2.cloned.1.call-start = ((), (), s32[]{:S(2)}) async-start(), calls=%async_computation.5 | async-start | bytes 17039360 | tf_op jit(solution)/shard_map/all_gather | solution.py:156
  9.1 5.6 %collective-permute-start.3 = (bf16[256,256]{1,0:T(8,128)(2,1)}, bf16[256,256]{1,0:T(8,128)(2,1)}, u32[]{:S(2)}, u32[]{:S(2)}) collective-permute-start(bf16[256,256]{1,0:T(8,128)(2,1)} %get-tuple-element.12), channel_id=1, source_target_pairs={{0,128},{128,0},{1,129},{129,1},{2,130},{130,2},{3,131},{131,3},{4... | collective-permute-start | bytes 393224 | tf_op jit(solution)/shard_map/ppermute | solution.py:154
  16.4 59.0 %collective-permute-start = (bf16[128,8192]{1,0:T(8,128)(2,1)}, bf16[128,8192]{1,0:T(8,128)(2,1)}, u32[]{:S(2)}, u32[]{:S(2)}) collective-permute-start(bf16[128,8192]{1,0:T(8,128)(2,1)} %refs_0_.1), channel_id=1, source_target_pairs={{0,128},{128,1},{1,129},{129,0},{2,130},{130,3},{3,131},{131,2},{4... | collective-permute-start | bytes 6291464 | tf_op jit(solution)/shard_map/ppermute | solution.py:28
  18.0 57.3 %collective-permute-start.1 = (bf16[128,8192]{1,0:T(8,128)(2,1)}, bf16[128,8192]{1,0:T(8,128)(2,1)}, u32[]{:S(2)}, u32[]{:S(2)}) collective-permute-start(bf16[128,8192]{1,0:T(8,128)(2,1)} %refs_0_.1), channel_id=1, source_target_pairs={{0,129},{128,0},{1,128},{129,1},{2,131},{130,2},{3,130},{131,3},{4... | collective-permute-start | bytes 6291464 | tf_op jit(solution)/shard_map/ppermute | solution.py:28
  25.5 79.0 %copy-start.4 = (s32[4]{0:T(128)S(1)}, s32[4]{0:T(128)}, u32[]{:S(2)}) copy-start(s32[4]{0:T(128)} %constant.42) | copy-start | bytes 52
  75.4 48.7 %collective-permute-start.2 = (bf16[128,8192]{1,0:T(8,128)(2,1)S(1)}, bf16[128,8192]{1,0:T(8,128)(2,1)}, u32[]{:S(2)}, u32[]{:S(2)}) collective-permute-start(bf16[128,8192]{1,0:T(8,128)(2,1)S(1)} %copy-done.1), channel_id=1, source_target_pairs={{0,1},{128,129},{1,0},{129,128},{2,3},{130,131},{3,2},{131,130},{4... | collective-permute-start | bytes 6291464 | tf_op jit(solution)/shard_map/ppermute | solution.py:28
  77.2 21.4 %all-to-all-start.2 = ((f32[32,1,768]{2,1,0:T(1,128)}), f32[32,1,768]{2,1,0:T(1,128)S(1)}, u32[]{:S(2)}, u32[]{:S(2)}) async-start(f32[32,1,768]{2,1,0:T(1,128)} %reshape.81), calls=%async_computation.2 | async-start | bytes 196608 | tf_op jit(solution)/shard_map/all_to_all | solution.py:40
  99.4 14.8 %all-to-all-start.3 = ((f32[32,1,768]{2,1,0:T(1,128)}), f32[32,1,768]{2,1,0:T(1,128)S(1)}, u32[]{:S(2)}, u32[]{:S(2)}) async-start(f32[32,1,768]{2,1,0:T(1,128)} %broadcast_in_dim.6), calls=%async_computation.3 | async-start | bytes 196608 | tf_op jit(solution)/shard_map/all_to_all | solution.py:24
  115.4 24.6 %all-to-all-start.4 = ((f32[8,16,1536]{2,1,0:T(8,128)}), f32[8,16,1536]{2,1,0:T(8,128)}, u32[]{:S(2)}, u32[]{:S(2)}) async-start(f32[8,16,1536]{2,1,0:T(8,128)} %broadcast_in_dim.15), calls=%async_computation.4 | async-start | bytes 1572864 | tf_op jit(solution)/shard_map/all_to_all | solution.py:24
  139.0 1.0 copy-start.2
  140.0 17.9 %all-to-all-start.1 = ((bf16[4,128,1024]{2,1,0:T(8,128)(2,1)}), bf16[4,128,1024]{2,1,0:T(8,128)(2,1)S(1)}, u32[]{:S(2)}, u32[]{:S(2)}) async-start(bf16[4,128,1024]{2,1,0:T(8,128)(2,1)} %copy-done.2), calls=%async_computation.1 | async-start | bytes 2097152 | tf_op jit(solution)/shard_map/all_to_all | solution.py:169
Sparse Core Ops, SparseCore 0:
  16.5 105.5 all-gather.1

commit v4 on v3

v4 whole, which is shorter than its diff:
```python
import functools
import math

import jax
import jax.numpy as jnp
from jax import lax
from jax.experimental import pallas as pl
from jax.experimental.pallas import tpu as pltpu
from jax.sharding import Mesh, PartitionSpec as P

GROUP = ("yhi", "ylo", "core")
REST = ("x", "z")
TOKENS = ("ylo", "z", "core", "x", "yhi")
HOPS = (0, 1, 3, 2)
F32 = jnp.float32


def place_of(y):
    return 2 * (y % 2) + y // 2


def gather_by_exchange(value, axes, n):
    return lax.all_to_all(jnp.broadcast_to(value[None], (n, *value.shape)), axes, 0, 0, tiled=True)


def along_y(value, hop):
    return lax.ppermute(value, ("ylo", "yhi"), [(place_of(i), place_of((i + hop) % 4)) for i in range(4)])


def scatter_group(part_down, part_up):
    rank = part_down.shape[0]
    both = jnp.concatenate([part_down, part_up], axis=1)
    width = both.shape[1]
    both = both.reshape(rank, 8, width // 8).transpose(1, 0, 2)
    return jnp.sum(lax.all_to_all(both, GROUP, 0, 0, tiled=True), axis=0)


def scatter_rest(mine):
    return lax.all_to_all(mine.reshape(32, 1, mine.size // 32), REST, 0, 0, tiled=True)


def gather_adapter(terms, rank, split):
    width = terms.size * 8 // rank
    mine = gather_by_exchange(jnp.sum(terms, axis=0), REST, 32).reshape(rank, width // 8)
    both = gather_by_exchange(mine, GROUP, 8)
    both = both.transpose(1, 0, 2).reshape(rank, width)
    return both[:, :split], both[:, split:]


def product_kernel(count, *refs):
    blocks, w, outs, (a_all, w_all, total, a_sem, w_sem) = refs[:count], refs[count], refs[count + 1 : 2 * count + 1], refs[2 * count + 1 :]
    rows, k = blocks[0].shape
    parts, _, kc, depth = w.shape
    wide = depth // 2

    def w_copy(i):
        return pltpu.make_async_copy(w.at[i], w_all.at[i], w_sem.at[i])

    def a_copies(part):
        for j, block in enumerate(blocks):
            for ylo in range(2):
                columns = pl.ds(ylo * (k // 2) + part * 4 * wide, 4 * wide)
                target = a_all.at[pl.ds(j * rows, rows), columns]
                yield pltpu.make_async_copy(block.at[:, columns], target, a_sem.at[part, 2 * j + ylo])

    for part in range(parts // 4):
        for copy in a_copies(part):
            copy.start()
        for i in range(4):
            w_copy(4 * part + i).start()

    def term(i, ylo):
        a = a_all[:, pl.ds(pl.multiple_of(ylo * (k // 2) + i * wide, wide), wide)]
        b = w_all[i, :, :, ylo * wide : (ylo + 1) * wide].reshape(4 * kc, wide)
        return lax.dot_general(a, b, (((1,), (1,)), ((), ())), preferred_element_type=F32)

    for part in range(parts // 4):
        for copy in a_copies(part):
            copy.wait()

        @pl.loop(0, 2)
        def _(half):
            first = 4 * part + 2 * half
            for i in range(2):
                w_copy(first + i).wait()
            here = sum(term(first + i, ylo) for i in range(2) for ylo in range(2))
            if part == 0:

                @pl.when(half == 0)
                def _():
                    total[...] = here

                @pl.when(half == 1)
                def _():
                    total[...] += here

            else:
                total[...] += here

    for j, out in enumerate(outs):
        out[...] = total[j * rows : (j + 1) * rows].astype(out.dtype)


def product(blocks, w):
    rows, k = blocks[0].shape
    parts, _, kc, depth = w.shape
    n = len(blocks)
    return pl.pallas_call(
        functools.partial(product_kernel, n),
        out_shape=[jax.ShapeDtypeStruct((rows, 4 * kc), jnp.bfloat16)] * n,
        in_specs=[pl.BlockSpec(memory_space=pl.ANY)] * (n + 1),
        out_specs=[pl.BlockSpec(memory_space=pltpu.VMEM)] * n,
        scratch_shapes=[
            pltpu.VMEM((n * rows, k), jnp.bfloat16),
            pltpu.VMEM((parts, 4, kc, depth), jnp.bfloat16),
            pltpu.VMEM((n * rows, 4 * kc), F32),
            pltpu.SemaphoreType.DMA((parts // 4, 2 * n)),
            pltpu.SemaphoreType.DMA((parts,)),
        ],
        compiler_params=pltpu.CompilerParams(vmem_limit_bytes=48 * 2**20),
        cost_estimate=pl.CostEstimate(
            flops=8 * n * rows * kc * k,
            bytes_accessed=2 * (n * rows * k + 4 * kc * k + 4 * n * rows * kc),
            transcendentals=0,
        ),
    )(*blocks, w)


def finish_kernel(place, *refs):
    parts, (back_low, down, out) = refs[:4], refs[4:]
    kc = parts[0].shape[1] // 4
    lowrank = 2.0 * jnp.dot(back_low[...], down[...], preferred_element_type=F32)
    for y in range(4):

        @pl.when(place[0] == y)
        def _():
            for hop, part in zip(HOPS, parts):
                for x in range(4):
                    at = (4 * x + (y + hop) % 4) * kc
                    columns = slice(at, at + kc)
                    frozen = part[:, x * kc : (x + 1) * kc].astype(F32)
                    out[:, columns] = (frozen + lowrank[:, columns]).astype(out.dtype)


def finish(place, parts, back_low, down):
    rows, rank = back_low.shape
    hd = down.shape[1]
    step = rows // 4
    return pl.pallas_call(
        finish_kernel,
        grid=(4,),
        out_shape=jax.ShapeDtypeStruct((rows, hd), jnp.bfloat16),
        in_specs=[pl.BlockSpec(memory_space=pltpu.SMEM)]
        + [pl.BlockSpec((step, hd // 4), lambda i: (i, 0))] * 4
        + [pl.BlockSpec((step, rank), lambda i: (i, 0)), pl.BlockSpec((rank, hd), lambda i: (0, 0))],
        out_specs=pl.BlockSpec((step, hd), lambda i: (i, 0)),
        compiler_params=pltpu.CompilerParams(vmem_limit_bytes=32 * 2**20),
        cost_estimate=pl.CostEstimate(flops=2 * rows * rank * hd, bytes_accessed=4 * rows * hd, transcendentals=0),
    )(place, *parts, back_low, down)


def local(acts, grads_out, base_output_weight, down_adapter_matrix, b_up):
    rows, hd = acts.shape
    d = grads_out.shape[1]
    norm_factor = 2.0 / math.sqrt(rows * 256)
    ylo = lax.axis_index("ylo")
    y = 2 * lax.axis_index("yhi") + ylo
    half = base_output_weight.shape[0] // 2
    mine = lax.dynamic_slice_in_dim(base_output_weight, ylo * half, half, 0)
    other = lax.dynamic_slice_in_dim(base_output_weight, (1 - ylo) * half, half, 0)
    other = lax.ppermute(other, "ylo", [(0, 1), (1, 0)])
    w = jnp.where(ylo == 0, jnp.concatenate([mine, other], axis=1), jnp.concatenate([other, mine], axis=1))
    w = lax.all_gather(w, ("z", "core", "x"), axis=0, tiled=False).reshape(16, 4, *w.shape)
    near = [along_y(grads_out, hop) for hop in HOPS[1:3]]

    low = jnp.einsum("tk,rk->tr", acts, down_adapter_matrix, preferred_element_type=F32).astype(jnp.bfloat16)
    back_low = jnp.einsum("td,rd->tr", grads_out, b_up, preferred_element_type=F32).astype(jnp.bfloat16)
    part_down = norm_factor * jnp.einsum("tr,tk->rk", back_low, acts, preferred_element_type=F32)
    part_up = norm_factor * jnp.einsum("tr,td->rd", low, grads_out, preferred_element_type=F32)
    total = scatter_group(part_down, part_up)
    total, far, *near = lax.optimization_barrier((total, grads_out, *near))
    blocks = [grads_out, *near, along_y(far, HOPS[3])]
    terms = scatter_rest(total)

    own, near_up, near_down, far = blocks
    from_far, from_up, from_down = product([far, near_up, near_down], w)
    (from_own,) = product([own], w)
    parts = [from_own, along_y(from_up, HOPS[2]), along_y(from_down, HOPS[1]), along_y(from_far, HOPS[3])]
    place = y.astype(jnp.int32)[None]
    grad_down, grad_up = gather_adapter(terms, low.shape[1], hd)
    return finish(place, parts, back_low, down_adapter_matrix), grad_down, grad_up


def solution(mesh):
    fine = Mesh(mesh.devices.reshape(2, 8, 2, 4, 2), ("ylo", "z", "core", "x", "yhi"))
    in_specs = (
        P(TOKENS, None),
        P(TOKENS, None),
        P(("x", "yhi"), ("ylo", "z", "core")),
        P(),
        P(),
    )
    out_specs = (P(TOKENS, None), P(), P())
    return jax.shard_map(local, mesh=fine, in_specs=in_specs, out_specs=out_specs, check_vma=False)
```

time: 169 us -> 163 us (0.964)
  blocking collectives: 48.6 us -> 84.3 us
  waiting for transfers between devices: 39.3 us -> 11.5 us
  starting transfers between devices: 30.6 us -> 13.9 us
  Pallas kernels: 17.1 us -> 24 us
  local copies, waits for them, and re-layouts: 8.02 us -> 5.77 us
    all_to_all x0 -> x2, blocking collectives: none -> 35.7 us  [the longest x1 21.1 us: scatter_rest(): lax.all_to_all(mine.reshape(32, 1, mine.size // 32), REST, 0, 0, tiled=True)]
    all_to_all x2 -> x0, waiting for transfers between devices: 21.3 us -> none  [the longest x1 11.6 us: local(): parts = lax.all_to_all(parts, Y, 0, 0, tiled=True)]
    all_to_all x2 -> x0, starting transfers between devices: 15.1 us -> none  [the longest x1 11.6 us: scatter_rest(): lax.all_to_all(mine.reshape(32, 1, mine.size // 32), REST, 0, 0, tiled=True)]
    all_to_all x2 -> x1, waiting for transfers between devices: 9.59 us -> 0.01 us  [gather_by_exchange(): lax.all_to_all(jnp.broadcast_to(value[None], (n, *value.shape)), axes, 0,...]
    pallas_call x1 -> x2, Pallas kernels: 15 us -> 20.2 us  [product(): pl.pallas_call(functools.partial(product_kernel, n), out_shape=[jax.Shape...]
    all_to_all x2 -> x1, starting transfers between devices: 9.4 us -> 4.24 us  [gather_by_exchange(): lax.all_to_all(jnp.broadcast_to(value[None], (n, *value.shape)), axes, 0,...]
    ppermute x3 -> x6, starting transfers between devices: 4.44 us -> 8.05 us  [along_y(): lax.ppermute(value, ('ylo', 'yhi'), [(place_of(i), place_of((i + hop) % 4...]
    ppermute x3 -> x6, waiting for transfers between devices: 4.41 us -> 7.62 us  [along_y(): lax.ppermute(value, ('ylo', 'yhi'), [(place_of(i), place_of((i + hop) % 4...]
  transfers between devices with their start and end apart: 9 -> 9, of which waited for: 5 -> 3; matrix products, arithmetic and copies ran while one was open for 8% -> 7% of each run, Pallas kernels for 9% -> 13%
where the time goes in v4:
time: 163 us; the launch traced here: 162 us
  blocking collectives  84.3 us (52%)
  Pallas kernels  24 us (15%)
  between operations  14.2 us (9%)
  starting transfers between devices  13.9 us (9%)
  waiting for transfers between devices  11.5 us (7%)
  local copies, waits for them, and re-layouts  5.77 us (4%)
  matrix products  4.68 us (3%)
  other arithmetic  3.41 us (2%)
    all_to_all x1, blocking collectives, scatter_group(): return jnp.sum(lax.all_to_all(both, GROUP, 0, 0, tiled=True), axis=0)  48.6 us
    all_to_all x1, blocking collectives, scatter_rest(): lax.all_to_all(mine.reshape(32, 1, mine.size // 32), REST, 0, 0, tiled=True)  21.1 us
    pallas_call x2, Pallas kernels, product(): pl.pallas_call(functools.partial(product_kernel, n), out_shape=[jax.Shape...  20.2 us
    all_to_all x1, blocking collectives, gather_by_exchange(): lax.all_to_all(jnp.broadcast_to(value[None], (n, *value.shape)), axes, 0,...  14.6 us
    ppermute x6, starting transfers between devices, along_y(): lax.ppermute(value, ('ylo', 'yhi'), [(place_of(i), place_of((i + hop) % 4...  8.05 us
    ppermute x6, waiting for transfers between devices, along_y(): lax.ppermute(value, ('ylo', 'yhi'), [(place_of(i), place_of((i + hop) % 4...  7.62 us
    all_to_all x1, starting transfers between devices, gather_by_exchange(): lax.all_to_all(jnp.broadcast_to(value[None], (n, *value.shape)), axes, 0,...  4.24 us
    ppermute x1, waiting for transfers between devices, local(): other = lax.ppermute(other, 'ylo', [(0, 1), (1, 0)])  3.87 us
  transfers between devices with their start and end apart: 9, of which 3 were waited for; matrix products, arithmetic and copies ran while one was open for 7% of the time, Pallas kernels for 13%

profile of v4, /device:TPU:2, one launch (start us, length us, event | category | flops | bytes accessed | tf_op | source)
XLA Modules:
  0.0 161.7 jit_solution(6566300991367461905)
XLA Ops:
  7.3 1.8 %dynamic-slice_bitcast_fusion = (bf16[1,256,256]{2,1,0:T(8,128)(2,1)S(1)}, bf16[256,256]{1,0:T(8,128)(2,1)}) fusion(bf16[512,256]{1,0:T(8,128)(2,1)} %param.7, s32[]{:T(128)S(6)} %select_n.22, s32[]{:T(128)S(6)} %select_n.23), kind=kLoop, calls=%fused_computation.7 | loop fusion | bytes 524296 | tf_op jit(solution)/shard_map/concatenate | solution.py:172
  9.1 1.6 collective-permute-start
  10.6 3.9 %collective-permute-done = bf16[256,256]{1,0:T(8,128)(2,1)S(1)} collective-permute-done((bf16[256,256]{1,0:T(8,128)(2,1)}, bf16[256,256]{1,0:T(8,128)(2,1)S(1)}, u32[]{:S(2)}, u32[]{:S(2)}) %collective-permute-start) | collective-permute-done | bytes 131104 | tf_op jit(solution)/shard_map/ppermute | solution.py:171
  14.5 0.8 maximum_select_fusion
  15.3 1.7 %collective-permute-start.1 = (bf16[128,8192]{1,0:T(8,128)(2,1)}, bf16[128,8192]{1,0:T(8,128)(2,1)}, u32[]{:S(2)}, u32[]{:S(2)}) collective-permute-start(bf16[128,8192]{1,0:T(8,128)(2,1)} %refs_0_.1), channel_id=1, source_target_pairs={{0,128},{128,1},{1,129},{129,0},{2,130},{130,3},{3,131},{131,2},{4... | collective-permute-start | bytes 6291464 | tf_op jit(solution)/shard_map/ppermute | solution.py:27
  17.0 1.7 %collective-permute-start.2 = (bf16[128,8192]{1,0:T(8,128)(2,1)}, bf16[128,8192]{1,0:T(8,128)(2,1)}, u32[]{:S(2)}, u32[]{:S(2)}) collective-permute-start(bf16[128,8192]{1,0:T(8,128)(2,1)} %refs_0_.1), channel_id=1, source_target_pairs={{0,129},{128,0},{1,128},{129,1},{2,131},{130,2},{3,130},{131,3},{4... | collective-permute-start | bytes 6291464 | tf_op jit(solution)/shard_map/ppermute | solution.py:27
  18.7 2.3 %convolution_convert_fusion.refs_4_ = bf16[128,16]{1,0:T(8,128)(2,1)S(1)} fusion(bf16[128,8192]{1,0:T(8,128)(2,1)} %refs_0_.1, bf16[16,8192]{1,0:T(8,128)(2,1)} %param.9), kind=kOutput, calls=%fused_computation.2 | convolution fusion | flops 33556480 | bytes 2363392 | tf_op jit(solution)/shard_map/td,rd->tr/dot_general | solution.py:177
  21.0 2.1 %convolution_multiply_fusion = f32[16,8192]{1,0:T(8,128)} fusion(bf16[128,8192]{1,0:T(8,128)(2,1)S(1)} %copy-done.1, bf16[128,4096]{1,0:T(8,128)(2,1)S(1)} %copy-done, bf16[16,4096]{1,0:T(8,128)(2,1)S(1)} %copy-done.2), kind=kOutput, calls=%fused_computation | convolution fusion | flops 50464768 | bytes 3801088 | tf_op jit(solution)/shard_map/tr,td->rd/dot_general | solution.py:179
  23.4 1.1 pad_maximum_fusion
  24.6 48.6 %all_to_all.20 = f32[8,16,1536]{2,1,0:T(8,128)} all-to-all(f32[8,16,1536]{2,1,0:T(8,128)S(1)} %bitcast.27), channel_id=1, replica_groups=mesh['ylo'=2,'z'=8,'core'=2,'x'=4,'yhi'=2] {'yhi','ylo','core'}, dimensions={0} | all-to-all | bytes 1572864 | tf_op jit(solution)/shard_map/all_to_all | solution.py:35
  73.1 1.2 reduce_sum.18
  74.3 1.1 collective-permute-start.3
  75.6 21.1 %all_to_all.21 = f32[32,1,768]{2,1,0:T(1,128)S(1)} all-to-all(f32[32,1,768]{2,1,0:T(1,128)S(1)} %reshape.81), channel_id=1, replica_groups=mesh['ylo'=2,'z'=8,'core'=2,'x'=4,'yhi'=2] {'x','z'}, dimensions={0} | all-to-all | bytes 196608 | tf_op jit(solution)/shard_map/all_to_all | solution.py:39
  96.9 14.6 %all_to_all.22 = f32[32,1,768]{2,1,0:T(1,128)S(1)} all-to-all(f32[32,1,768]{2,1,0:T(1,128)S(1)} %broadcast_in_dim.17), channel_id=1, replica_groups=mesh['ylo'=2,'z'=8,'core'=2,'x'=4,'yhi'=2] {'x','z'}, dimensions={0} | all-to-all | bytes 196608 | tf_op jit(solution)/shard_map/all_to_all | solution.py:23
  111.7 1.0 broadcast_in_dim.19
  112.7 4.2 %all-to-all-start.3 = ((f32[8,16,1536]{2,1,0:T(8,128)}), f32[8,16,1536]{2,1,0:T(8,128)}, u32[]{:S(2)}, u32[]{:S(2)}) async-start(f32[8,16,1536]{2,1,0:T(8,128)} %broadcast_in_dim.19), calls=%async_computation.3 | async-start | bytes 1572864 | tf_op jit(solution)/shard_map/all_to_all | solution.py:23
  116.9 7.5 %collective-permute-done.3.refs_0_ = bf16[128,8192]{1,0:T(8,128)(2,1)} collective-permute-done((bf16[128,8192]{1,0:T(8,128)(2,1)S(1)}, bf16[128,8192]{1,0:T(8,128)(2,1)}, u32[]{:S(2)}, u32[]{:S(2)}) %collective-permute-start.3) | collective-permute-done | bytes 2097184 | tf_op jit(solution)/shard_map/ppermute | solution.py:27
  124.4 11.9 %shard_map.77 = (bf16[128,1024]{1,0:T(8,128)(2,1)}, bf16[128,1024]{1,0:T(8,128)(2,1)}, bf16[128,1024]{1,0:T(8,128)(2,1)}) custom-call(bf16[128,8192]{1,0:T(8,128)(2,1)} %collective-permute-done.3.refs_0_, bf16[128,8192]{1,0:T(8,128)(2,1)} %collective-permute-done.1.refs_1_, bf16[128,8192]{1,0:T(8,128)(2,1)} %collective-permute-done.2.refs_2_, ...), custom_call_target="tpu_custom_call" | custom-call | flops 6442450944 | bytes 23855104 | tf_op jit(solution)/shard_map/pallas_call | solution.py:108
  136.3 2.0 %collective-permute-start.4 = (bf16[128,1024]{1,0:T(8,128)(2,1)}, bf16[128,1024]{1,0:T(8,128)(2,1)S(1)}, u32[]{:S(2)}, u32[]{:S(2)}) collective-permute-start(bf16[128,1024]{1,0:T(8,128)(2,1)} %get-tuple-element.13), channel_id=1, source_target_pairs={{0,129},{128,0},{1,128},{129,1},{2,131},{130,2},{3,130},{131,3},{4... | collective-permute-start | bytes 786440 | tf_op jit(solution)/shard_map/ppermute | solution.py:27
  138.4 1.5 collective-permute-start.6
  139.9 1.2 copy.16
  141.1 0.8 slice.9
  142.6 8.4 %shard_map.76.refs_0_ = bf16[128,1024]{1,0:T(8,128)(2,1)S(1)} custom-call(bf16[128,8192]{1,0:T(8,128)(2,1)S(1)} %copy-done.1, bf16[16,4,256,512]{3,2,1,0:T(8,128)(2,1)} %bitcast.23), custom_call_target="tpu_custom_call" | custom-call | flops 2147483648 | bytes 19136512 | tf_op jit(solution)/shard_map/pallas_call | solution.py:108
  151.1 3.7 %shard_map.78 = bf16[128,4096]{1,0:T(8,128)(2,1)} custom-call(s32[1]{0:T(128)} %bitcast.place, bf16[128,1024]{1,0:T(8,128)(2,1)S(1)} %shard_map.76.refs_0_, bf16[128,1024]{1,0:T(8,128)(2,1)S(1)} %collective-permute-done.4.refs_1_, bf16[128,1024]{1,0:T(8,128)(2,1)} %collective-permute-done.5.refs_2_, bf16[128,1024]{1,0:T(8,128)(2,1)} %collective-permute-done.6.refs_3_, ...), custom_call_target="tpu_custom_call" | custom-call | flops 16777216 | bytes 2097152 | tf_op jit(solution)/shard_map/pallas_call | solution.py:149
  (28 shorter events, 1.8 us)
Async XLA Ops:
  7.2 13.8 %copy-start = (bf16[128,4096]{1,0:T(8,128)(2,1)S(1)}, bf16[128,4096]{1,0:T(8,128)(2,1)}, u32[]{:S(2)}) copy-start(bf16[128,4096]{1,0:T(8,128)(2,1)} %param.5) | copy-start | bytes 3145732
  7.2 13.8 %copy-start.1 = (bf16[128,8192]{1,0:T(8,128)(2,1)S(1)}, bf16[128,8192]{1,0:T(8,128)(2,1)}, u32[]{:S(2)}) copy-start(bf16[128,8192]{1,0:T(8,128)(2,1)} %refs_0_.1) | copy-start | bytes 6291460
  7.2 13.8 %copy-start.2 = (bf16[16,4096]{1,0:T(8,128)(2,1)S(1)}, bf16[16,4096]{1,0:T(8,128)(2,1)}, u32[]{:S(2)}) copy-start(bf16[16,4096]{1,0:T(8,128)(2,1)} %refs_5_.1) | copy-start | bytes 393220
  7.2 117.2 %all-gather.2.cloned.1.call-start = ((), (), s32[]{:S(2)}) async-start(), calls=%async_computation.4 | async-start | bytes 17039360 | tf_op jit(solution)/shard_map/all_gather | solution.py:173
  9.1 5.4 %collective-permute-start = (bf16[256,256]{1,0:T(8,128)(2,1)}, bf16[256,256]{1,0:T(8,128)(2,1)S(1)}, u32[]{:S(2)}, u32[]{:S(2)}) collective-permute-start(bf16[256,256]{1,0:T(8,128)(2,1)} %get-tuple-element.18), channel_id=1, source_target_pairs={{0,128},{128,0},{1,129},{129,1},{2,130},{130,2},{3,131},{131,3},{4... | collective-permute-start | bytes 393224 | tf_op jit(solution)/shard_map/ppermute | solution.py:171
  15.3 59.0 %collective-permute-start.1 = (bf16[128,8192]{1,0:T(8,128)(2,1)}, bf16[128,8192]{1,0:T(8,128)(2,1)}, u32[]{:S(2)}, u32[]{:S(2)}) collective-permute-start(bf16[128,8192]{1,0:T(8,128)(2,1)} %refs_0_.1), channel_id=1, source_target_pairs={{0,128},{128,1},{1,129},{129,0},{2,130},{130,3},{3,131},{131,2},{4... | collective-permute-start | bytes 6291464 | tf_op jit(solution)/shard_map/ppermute | solution.py:27
  17.0 57.3 %collective-permute-start.2 = (bf16[128,8192]{1,0:T(8,128)(2,1)}, bf16[128,8192]{1,0:T(8,128)(2,1)}, u32[]{:S(2)}, u32[]{:S(2)}) collective-permute-start(bf16[128,8192]{1,0:T(8,128)(2,1)} %refs_0_.1), channel_id=1, source_target_pairs={{0,129},{128,0},{1,128},{129,1},{2,131},{130,2},{3,130},{131,3},{4... | collective-permute-start | bytes 6291464 | tf_op jit(solution)/shard_map/ppermute | solution.py:27
  21.0 2.4 %copy-start.3 = (bf16[128,16]{1,0:T(8,128)(2,1)}, bf16[128,16]{1,0:T(8,128)(2,1)S(1)}, u32[]{:S(2)}) copy-start(bf16[128,16]{1,0:T(8,128)(2,1)S(1)} %convolution_convert_fusion.refs_4_) | copy-start | bytes 12292
  74.3 50.1 %collective-permute-start.3 = (bf16[128,8192]{1,0:T(8,128)(2,1)S(1)}, bf16[128,8192]{1,0:T(8,128)(2,1)}, u32[]{:S(2)}, u32[]{:S(2)}) collective-permute-start(bf16[128,8192]{1,0:T(8,128)(2,1)S(1)} %copy-done.1), channel_id=1, source_target_pairs={{0,1},{128,129},{1,0},{129,128},{2,3},{130,131},{3,2},{131,130},{4... | collective-permute-start | bytes 6291464 | tf_op jit(solution)/shard_map/ppermute | solution.py:27
  112.7 27.2 %all-to-all-start.3 = ((f32[8,16,1536]{2,1,0:T(8,128)}), f32[8,16,1536]{2,1,0:T(8,128)}, u32[]{:S(2)}, u32[]{:S(2)}) async-start(f32[8,16,1536]{2,1,0:T(8,128)} %broadcast_in_dim.19), calls=%async_computation.3 | async-start | bytes 1572864 | tf_op jit(solution)/shard_map/all_to_all | solution.py:23
  136.3 14.7 %collective-permute-start.4 = (bf16[128,1024]{1,0:T(8,128)(2,1)}, bf16[128,1024]{1,0:T(8,128)(2,1)S(1)}, u32[]{:S(2)}, u32[]{:S(2)}) collective-permute-start(bf16[128,1024]{1,0:T(8,128)(2,1)} %get-tuple-element.13), channel_id=1, source_target_pairs={{0,129},{128,0},{1,128},{129,1},{2,131},{130,2},{3,130},{131,3},{4... | collective-permute-start | bytes 786440 | tf_op jit(solution)/shard_map/ppermute | solution.py:27
  138.3 12.8 %collective-permute-start.5 = (bf16[128,1024]{1,0:T(8,128)(2,1)}, bf16[128,1024]{1,0:T(8,128)(2,1)}, u32[]{:S(2)}, u32[]{:S(2)}) collective-permute-start(bf16[128,1024]{1,0:T(8,128)(2,1)} %get-tuple-element.14), channel_id=1, source_target_pairs={{0,128},{128,1},{1,129},{129,0},{2,130},{130,3},{3,131},{131,2},{4... | collective-permute-start | bytes 786440 | tf_op jit(solution)/shard_map/ppermute | solution.py:27
  138.4 12.8 %collective-permute-start.6 = (bf16[128,1024]{1,0:T(8,128)(2,1)}, bf16[128,1024]{1,0:T(8,128)(2,1)}, u32[]{:S(2)}, u32[]{:S(2)}) collective-permute-start(bf16[128,1024]{1,0:T(8,128)(2,1)} %get-tuple-element.15), channel_id=1, source_target_pairs={{0,1},{128,129},{1,0},{129,128},{2,3},{130,131},{3,2},{131,130},{4... | collective-permute-start | bytes 786440 | tf_op jit(solution)/shard_map/ppermute | solution.py:27
  142.6 8.5 %copy-start.4 = (bf16[128,16]{1,0:T(8,128)(2,1)S(1)}, bf16[128,16]{1,0:T(8,128)(2,1)}, u32[]{:S(2)}) copy-start(bf16[128,16]{1,0:T(8,128)(2,1)} %copy-done.3) | copy-start | bytes 12292
Sparse Core Ops, SparseCore 0:
  15.5 105.5 all-gather.1

commit v5 on v4

--- a/solution.py
+++ b/solution.py
@@ -50,11 +50,11 @@
 def product_kernel(count, *refs):
     blocks, w, outs, (a_all, w_all, total, a_sem, w_sem) = refs[:count], refs[count], refs[count + 1 : 2 * count + 1], refs[2 * count + 1 :]
     rows, k = blocks[0].shape
-    parts, _, kc, depth = w.shape
+    _, parts, kc, depth = w.shape
     wide = depth // 2
 
     def w_copy(i):
-        return pltpu.make_async_copy(w.at[i], w_all.at[i], w_sem.at[i])
+        return pltpu.make_async_copy(w.at[:, i], w_all.at[i], w_sem.at[i])
 
     def a_copies(part):
         for j, block in enumerate(blocks):
@@ -103,7 +103,7 @@
 
 def product(blocks, w):
     rows, k = blocks[0].shape
-    parts, _, kc, depth = w.shape
+    _, parts, kc, depth = w.shape
     n = len(blocks)
     return pl.pallas_call(
         functools.partial(product_kernel, n),
@@ -145,10 +145,10 @@
 def finish(place, parts, back_low, down):
     rows, rank = back_low.shape
     hd = down.shape[1]
-    step = rows // 4
+    step = rows // 2
     return pl.pallas_call(
         finish_kernel,
-        grid=(4,),
+        grid=(2,),
         out_shape=jax.ShapeDtypeStruct((rows, hd), jnp.bfloat16),
         in_specs=[pl.BlockSpec(memory_space=pltpu.SMEM)]
         + [pl.BlockSpec((step, hd // 4), lambda i: (i, 0))] * 4
@@ -166,11 +166,12 @@
     ylo = lax.axis_index("ylo")
     y = 2 * lax.axis_index("yhi") + ylo
     half = base_output_weight.shape[0] // 2
-    mine = lax.dynamic_slice_in_dim(base_output_weight, ylo * half, half, 0)
     other = lax.dynamic_slice_in_dim(base_output_weight, (1 - ylo) * half, half, 0)
+    other, kept = lax.optimization_barrier((other, base_output_weight))
+    mine = lax.dynamic_slice_in_dim(kept, ylo * half, half, 0)
     other = lax.ppermute(other, "ylo", [(0, 1), (1, 0)])
     w = jnp.where(ylo == 0, jnp.concatenate([mine, other], axis=1), jnp.concatenate([other, mine], axis=1))
-    w = lax.all_gather(w, ("z", "core", "x"), axis=0, tiled=False).reshape(16, 4, *w.shape)
+    w = lax.all_gather(w, ("x", "z", "core"), axis=0, tiled=False).reshape(4, 16, *w.shape)
     near = [along_y(grads_out, hop) for hop in HOPS[1:3]]
 
     low = jnp.einsum("tk,rk->tr", acts, down_adapter_matrix, preferred_element_type=F32).astype(jnp.bfloat16)

time: 163 us -> 161 us (0.988)
  transfers between devices with their start and end apart: 9 -> 9, of which waited for: 3 -> 3; matrix products, arithmetic and copies ran while one was open for 7% -> 8% of each run, Pallas kernels for 13% -> 13%
where the time goes in v5:
time: 161 us; the launch traced here: 160 us
  blocking collectives  84.3 us (52%)
  Pallas kernels  22.8 us (14%)
  between operations  14.2 us (9%)
  starting transfers between devices  14 us (9%)
  waiting for transfers between devices  10.4 us (6%)
  local copies, waits for them, and re-layouts  5.95 us (4%)
  matrix products  4.68 us (3%)
  other arithmetic  3.41 us (2%)
    all_to_all x1, blocking collectives, scatter_group(): return jnp.sum(lax.all_to_all(both, GROUP, 0, 0, tiled=True), axis=0)  48.6 us
    all_to_all x1, blocking collectives, scatter_rest(): lax.all_to_all(mine.reshape(32, 1, mine.size // 32), REST, 0, 0, tiled=True)  21.1 us
    pallas_call x2, Pallas kernels, product(): pl.pallas_call(functools.partial(product_kernel, n), out_shape=[jax.Shape...  20.2 us
    all_to_all x1, blocking collectives, gather_by_exchange(): lax.all_to_all(jnp.broadcast_to(value[None], (n, *value.shape)), axes, 0,...  14.6 us
    ppermute x6, starting transfers between devices, along_y(): lax.ppermute(value, ('ylo', 'yhi'), [(place_of(i), place_of((i + hop) % 4...  8.04 us
    ppermute x6, waiting for transfers between devices, along_y(): lax.ppermute(value, ('ylo', 'yhi'), [(place_of(i), place_of((i + hop) % 4...  7.63 us
    all_to_all x1, starting transfers between devices, gather_by_exchange(): lax.all_to_all(jnp.broadcast_to(value[None], (n, *value.shape)), axes, 0,...  4.22 us
  transfers between devices with their start and end apart: 9, of which 3 were waited for; matrix products, arithmetic and copies ran while one was open for 8% of the time, Pallas kernels for 13%

profile of v5, /device:TPU:2, one launch (start us, length us, event | category | flops | bytes accessed | tf_op | source)
XLA Modules:
  0.0 159.7 jit_solution(6706925638360934137)
XLA Ops:
  7.3 1.1 constant_dynamic-slice_fusion
  8.3 1.7 %collective-permute-start = (bf16[256,256]{1,0:T(8,128)(2,1)S(1)}, bf16[256,256]{1,0:T(8,128)(2,1)S(1)}, u32[]{:S(2)}, u32[]{:S(2)}) collective-permute-start(bf16[256,256]{1,0:T(8,128)(2,1)S(1)} %constant_dynamic-slice_fusion), channel_id=1, source_target_pairs={{0,128},{128,0},{1,129},{129,1},{2,130},{130,2},{3,131},{131,3},{4... | collective-permute-start | bytes 393224 | tf_op jit(solution)/shard_map/ppermute | solution.py:172
  10.0 0.9 dynamic-slice_bitcast_fusion
  10.9 2.7 %collective-permute-done = bf16[256,256]{1,0:T(8,128)(2,1)S(1)} collective-permute-done((bf16[256,256]{1,0:T(8,128)(2,1)S(1)}, bf16[256,256]{1,0:T(8,128)(2,1)S(1)}, u32[]{:S(2)}, u32[]{:S(2)}) %collective-permute-start) | collective-permute-done | bytes 131104 | tf_op jit(solution)/shard_map/ppermute | solution.py:172
  14.5 1.7 %collective-permute-start.1 = (bf16[128,8192]{1,0:T(8,128)(2,1)}, bf16[128,8192]{1,0:T(8,128)(2,1)}, u32[]{:S(2)}, u32[]{:S(2)}) collective-permute-start(bf16[128,8192]{1,0:T(8,128)(2,1)} %refs_0_.1), channel_id=1, source_target_pairs={{0,128},{128,1},{1,129},{129,0},{2,130},{130,3},{3,131},{131,2},{4... | collective-permute-start | bytes 6291464 | tf_op jit(solution)/shard_map/ppermute | solution.py:27
  16.2 1.7 %collective-permute-start.2 = (bf16[128,8192]{1,0:T(8,128)(2,1)}, bf16[128,8192]{1,0:T(8,128)(2,1)}, u32[]{:S(2)}, u32[]{:S(2)}) collective-permute-start(bf16[128,8192]{1,0:T(8,128)(2,1)} %refs_0_.1), channel_id=1, source_target_pairs={{0,129},{128,0},{1,128},{129,1},{2,131},{130,2},{3,130},{131,3},{4... | collective-permute-start | bytes 6291464 | tf_op jit(solution)/shard_map/ppermute | solution.py:27
  17.8 2.3 %convolution_convert_fusion.refs_4_ = bf16[128,16]{1,0:T(8,128)(2,1)S(1)} fusion(bf16[128,8192]{1,0:T(8,128)(2,1)} %refs_0_.1, bf16[16,8192]{1,0:T(8,128)(2,1)} %param.9), kind=kOutput, calls=%fused_computation.2 | convolution fusion | flops 33556480 | bytes 2363392 | tf_op jit(solution)/shard_map/td,rd->tr/dot_general | solution.py:178
  20.2 2.1 %convolution_multiply_fusion = f32[16,8192]{1,0:T(8,128)} fusion(bf16[128,8192]{1,0:T(8,128)(2,1)S(1)} %copy-done.1, bf16[128,4096]{1,0:T(8,128)(2,1)S(1)} %copy-done, bf16[16,4096]{1,0:T(8,128)(2,1)S(1)} %copy-done.2), kind=kOutput, calls=%fused_computation | convolution fusion | flops 50464768 | bytes 3801088 | tf_op jit(solution)/shard_map/tr,td->rd/dot_general | solution.py:180
  22.5 1.1 pad_maximum_fusion
  23.7 48.6 %all_to_all.20 = f32[8,16,1536]{2,1,0:T(8,128)} all-to-all(f32[8,16,1536]{2,1,0:T(8,128)S(1)} %bitcast.27), channel_id=1, replica_groups=mesh['ylo'=2,'z'=8,'core'=2,'x'=4,'yhi'=2] {'yhi','ylo','core'}, dimensions={0} | all-to-all | bytes 1572864 | tf_op jit(solution)/shard_map/all_to_all | solution.py:35
  72.3 1.2 reduce_sum.18
  73.5 1.1 collective-permute-start.3
  74.7 21.1 %all_to_all.21 = f32[32,1,768]{2,1,0:T(1,128)S(1)} all-to-all(f32[32,1,768]{2,1,0:T(1,128)S(1)} %reshape.81), channel_id=1, replica_groups=mesh['ylo'=2,'z'=8,'core'=2,'x'=4,'yhi'=2] {'x','z'}, dimensions={0} | all-to-all | bytes 196608 | tf_op jit(solution)/shard_map/all_to_all | solution.py:39
  96.0 14.6 %all_to_all.22 = f32[32,1,768]{2,1,0:T(1,128)S(1)} all-to-all(f32[32,1,768]{2,1,0:T(1,128)S(1)} %broadcast_in_dim.17), channel_id=1, replica_groups=mesh['ylo'=2,'z'=8,'core'=2,'x'=4,'yhi'=2] {'x','z'}, dimensions={0} | all-to-all | bytes 196608 | tf_op jit(solution)/shard_map/all_to_all | solution.py:23
  110.9 1.0 broadcast_in_dim.19
  111.8 4.2 %all-to-all-start.3 = ((f32[8,16,1536]{2,1,0:T(8,128)}), f32[8,16,1536]{2,1,0:T(8,128)}, u32[]{:S(2)}, u32[]{:S(2)}) async-start(f32[8,16,1536]{2,1,0:T(8,128)} %broadcast_in_dim.19), calls=%async_computation.3 | async-start | bytes 1572864 | tf_op jit(solution)/shard_map/all_to_all | solution.py:23
  116.1 7.5 %collective-permute-done.3.refs_0_ = bf16[128,8192]{1,0:T(8,128)(2,1)} collective-permute-done((bf16[128,8192]{1,0:T(8,128)(2,1)S(1)}, bf16[128,8192]{1,0:T(8,128)(2,1)}, u32[]{:S(2)}, u32[]{:S(2)}) %collective-permute-start.3) | collective-permute-done | bytes 2097184 | tf_op jit(solution)/shard_map/ppermute | solution.py:27
  123.5 11.9 %shard_map.77 = (bf16[128,1024]{1,0:T(8,128)(2,1)}, bf16[128,1024]{1,0:T(8,128)(2,1)}, bf16[128,1024]{1,0:T(8,128)(2,1)}) custom-call(bf16[128,8192]{1,0:T(8,128)(2,1)} %collective-permute-done.3.refs_0_, bf16[128,8192]{1,0:T(8,128)(2,1)} %collective-permute-done.1.refs_1_, bf16[128,8192]{1,0:T(8,128)(2,1)} %collective-permute-done.2.refs_2_, ...), custom_call_target="tpu_custom_call" | custom-call | flops 6442450944 | bytes 23855104 | tf_op jit(solution)/shard_map/pallas_call | solution.py:108
  135.4 2.0 %collective-permute-start.4 = (bf16[128,1024]{1,0:T(8,128)(2,1)}, bf16[128,1024]{1,0:T(8,128)(2,1)S(1)}, u32[]{:S(2)}, u32[]{:S(2)}) collective-permute-start(bf16[128,1024]{1,0:T(8,128)(2,1)} %get-tuple-element.17), channel_id=1, source_target_pairs={{0,129},{128,0},{1,128},{129,1},{2,131},{130,2},{3,130},{131,3},{4... | collective-permute-start | bytes 786440 | tf_op jit(solution)/shard_map/ppermute | solution.py:27
  137.5 1.5 collective-permute-start.6
  139.0 1.2 copy.16
  140.2 0.8 slice.9
  141.7 8.4 %shard_map.76.refs_0_ = bf16[128,1024]{1,0:T(8,128)(2,1)S(1)} custom-call(bf16[128,8192]{1,0:T(8,128)(2,1)S(1)} %copy-done.1, bf16[4,16,256,512]{3,2,1,0:T(8,128)(2,1)} %bitcast.23), custom_call_target="tpu_custom_call" | custom-call | flops 2147483648 | bytes 19136512 | tf_op jit(solution)/shard_map/pallas_call | solution.py:108
  150.3 2.6 %shard_map.78 = bf16[128,4096]{1,0:T(8,128)(2,1)} custom-call(s32[1]{0:T(128)} %bitcast.place, bf16[128,1024]{1,0:T(8,128)(2,1)S(1)} %shard_map.76.refs_0_, bf16[128,1024]{1,0:T(8,128)(2,1)S(1)} %collective-permute-done.4.refs_1_, bf16[128,1024]{1,0:T(8,128)(2,1)} %collective-permute-done.5.refs_2_, bf16[128,1024]{1,0:T(8,128)(2,1)} %collective-permute-done.6.refs_3_, ...), custom_call_target="tpu_custom_call" | custom-call | flops 16777216 | bytes 2097152 | tf_op jit(solution)/shard_map/pallas_call | solution.py:149
  (29 shorter events, 2.7 us)
Async XLA Ops:
  7.2 13.0 %copy-start = (bf16[128,4096]{1,0:T(8,128)(2,1)S(1)}, bf16[128,4096]{1,0:T(8,128)(2,1)}, u32[]{:S(2)}) copy-start(bf16[128,4096]{1,0:T(8,128)(2,1)} %param.5) | copy-start | bytes 3145732
  7.2 13.0 %copy-start.1 = (bf16[128,8192]{1,0:T(8,128)(2,1)S(1)}, bf16[128,8192]{1,0:T(8,128)(2,1)}, u32[]{:S(2)}) copy-start(bf16[128,8192]{1,0:T(8,128)(2,1)} %refs_0_.1) | copy-start | bytes 6291460
  7.2 13.0 %copy-start.2 = (bf16[16,4096]{1,0:T(8,128)(2,1)S(1)}, bf16[16,4096]{1,0:T(8,128)(2,1)}, u32[]{:S(2)}) copy-start(bf16[16,4096]{1,0:T(8,128)(2,1)} %refs_5_.1) | copy-start | bytes 393220
  7.2 116.3 %all-gather.2.cloned.1.call-start = ((), (), s32[]{:S(2)}) async-start(), calls=%async_computation.4 | async-start | bytes 17039360 | tf_op jit(solution)/shard_map/all_gather | solution.py:174
  8.3 5.3 %collective-permute-start = (bf16[256,256]{1,0:T(8,128)(2,1)S(1)}, bf16[256,256]{1,0:T(8,128)(2,1)S(1)}, u32[]{:S(2)}, u32[]{:S(2)}) collective-permute-start(bf16[256,256]{1,0:T(8,128)(2,1)S(1)} %constant_dynamic-slice_fusion), channel_id=1, source_target_pairs={{0,128},{128,0},{1,129},{129,1},{2,130},{130,2},{3,131},{131,3},{4... | collective-permute-start | bytes 393224 | tf_op jit(solution)/shard_map/ppermute | solution.py:172
  14.5 59.0 %collective-permute-start.1 = (bf16[128,8192]{1,0:T(8,128)(2,1)}, bf16[128,8192]{1,0:T(8,128)(2,1)}, u32[]{:S(2)}, u32[]{:S(2)}) collective-permute-start(bf16[128,8192]{1,0:T(8,128)(2,1)} %refs_0_.1), channel_id=1, source_target_pairs={{0,128},{128,1},{1,129},{129,0},{2,130},{130,3},{3,131},{131,2},{4... | collective-permute-start | bytes 6291464 | tf_op jit(solution)/shard_map/ppermute | solution.py:27
  16.2 57.3 %collective-permute-start.2 = (bf16[128,8192]{1,0:T(8,128)(2,1)}, bf16[128,8192]{1,0:T(8,128)(2,1)}, u32[]{:S(2)}, u32[]{:S(2)}) collective-permute-start(bf16[128,8192]{1,0:T(8,128)(2,1)} %refs_0_.1), channel_id=1, source_target_pairs={{0,129},{128,0},{1,128},{129,1},{2,131},{130,2},{3,130},{131,3},{4... | collective-permute-start | bytes 6291464 | tf_op jit(solution)/shard_map/ppermute | solution.py:27
  20.1 2.4 %copy-start.3 = (bf16[128,16]{1,0:T(8,128)(2,1)}, bf16[128,16]{1,0:T(8,128)(2,1)S(1)}, u32[]{:S(2)}) copy-start(bf16[128,16]{1,0:T(8,128)(2,1)S(1)} %convolution_convert_fusion.refs_4_) | copy-start | bytes 12292
  73.5 50.1 %collective-permute-start.3 = (bf16[128,8192]{1,0:T(8,128)(2,1)S(1)}, bf16[128,8192]{1,0:T(8,128)(2,1)}, u32[]{:S(2)}, u32[]{:S(2)}) collective-permute-start(bf16[128,8192]{1,0:T(8,128)(2,1)S(1)} %copy-done.1), channel_id=1, source_target_pairs={{0,1},{128,129},{1,0},{129,128},{2,3},{130,131},{3,2},{131,130},{4... | collective-permute-start | bytes 6291464 | tf_op jit(solution)/shard_map/ppermute | solution.py:27
  111.8 27.2 %all-to-all-start.3 = ((f32[8,16,1536]{2,1,0:T(8,128)}), f32[8,16,1536]{2,1,0:T(8,128)}, u32[]{:S(2)}, u32[]{:S(2)}) async-start(f32[8,16,1536]{2,1,0:T(8,128)} %broadcast_in_dim.19), calls=%async_computation.3 | async-start | bytes 1572864 | tf_op jit(solution)/shard_map/all_to_all | solution.py:23
  135.4 14.7 %collective-permute-start.4 = (bf16[128,1024]{1,0:T(8,128)(2,1)}, bf16[128,1024]{1,0:T(8,128)(2,1)S(1)}, u32[]{:S(2)}, u32[]{:S(2)}) collective-permute-start(bf16[128,1024]{1,0:T(8,128)(2,1)} %get-tuple-element.17), channel_id=1, source_target_pairs={{0,129},{128,0},{1,128},{129,1},{2,131},{130,2},{3,130},{131,3},{4... | collective-permute-start | bytes 786440 | tf_op jit(solution)/shard_map/ppermute | solution.py:27
  137.4 12.8 %collective-permute-start.5 = (bf16[128,1024]{1,0:T(8,128)(2,1)}, bf16[128,1024]{1,0:T(8,128)(2,1)}, u32[]{:S(2)}, u32[]{:S(2)}) collective-permute-start(bf16[128,1024]{1,0:T(8,128)(2,1)} %get-tuple-element.18), channel_id=1, source_target_pairs={{0,128},{128,1},{1,129},{129,0},{2,130},{130,3},{3,131},{131,2},{4... | collective-permute-start | bytes 786440 | tf_op jit(solution)/shard_map/ppermute | solution.py:27
  137.5 12.8 %collective-permute-start.6 = (bf16[128,1024]{1,0:T(8,128)(2,1)}, bf16[128,1024]{1,0:T(8,128)(2,1)}, u32[]{:S(2)}, u32[]{:S(2)}) collective-permute-start(bf16[128,1024]{1,0:T(8,128)(2,1)} %get-tuple-element.19), channel_id=1, source_target_pairs={{0,1},{128,129},{1,0},{129,128},{2,3},{130,131},{3,2},{131,130},{4... | collective-permute-start | bytes 786440 | tf_op jit(solution)/shard_map/ppermute | solution.py:27
  141.7 8.5 %copy-start.4 = (bf16[128,16]{1,0:T(8,128)(2,1)S(1)}, bf16[128,16]{1,0:T(8,128)(2,1)}, u32[]{:S(2)}) copy-start(bf16[128,16]{1,0:T(8,128)(2,1)} %copy-done.3) | copy-start | bytes 12292
Sparse Core Ops, SparseCore 0:
  14.6 105.5 all-gather.1

commit v6 on v5

--- a/solution.py
+++ b/solution.py
@@ -8,7 +8,7 @@
 from jax.experimental.pallas import tpu as pltpu
 from jax.sharding import Mesh, PartitionSpec as P
 
-GROUP = ("yhi", "ylo", "core")
+GROUP = ("core", "yhi", "ylo")
 REST = ("x", "z")
 TOKENS = ("ylo", "z", "core", "x", "yhi")
 HOPS = (0, 1, 3, 2)
@@ -27,12 +27,16 @@
     return lax.ppermute(value, ("ylo", "yhi"), [(place_of(i), place_of((i + hop) % 4)) for i in range(4)])
 
 
-def scatter_group(part_down, part_up):
-    rank = part_down.shape[0]
+def scatter_group(part_down, part_up, y, core):
     both = jnp.concatenate([part_down, part_up], axis=1)
-    width = both.shape[1]
-    both = both.reshape(rank, 8, width // 8).transpose(1, 0, 2)
-    return jnp.sum(lax.all_to_all(both, GROUP, 0, 0, tiled=True), axis=0)
+    width = both.shape[1] // 8
+    at = [4 * core * width, 4 * (1 - core) * width]
+    mine, other = (lax.dynamic_slice_in_dim(both, i, 4 * width, 1) for i in at)
+    mine = mine + lax.ppermute(other, "core", [(0, 1), (1, 0)])
+    total = lax.dynamic_slice_in_dim(mine, y * width, width, 1)
+    for hop in HOPS[1:]:
+        total = total + along_y(lax.dynamic_slice_in_dim(mine, (y + hop) % 4 * width, width, 1), hop)
+    return total
 
 
 def scatter_rest(mine):
@@ -178,7 +182,7 @@
     back_low = jnp.einsum("td,rd->tr", grads_out, b_up, preferred_element_type=F32).astype(jnp.bfloat16)
     part_down = norm_factor * jnp.einsum("tr,tk->rk", back_low, acts, preferred_element_type=F32)
     part_up = norm_factor * jnp.einsum("tr,td->rd", low, grads_out, preferred_element_type=F32)
-    total = scatter_group(part_down, part_up)
+    total = scatter_group(part_down, part_up, y, lax.axis_index("core"))
     total, far, *near = lax.optimization_barrier((total, grads_out, *near))
     blocks = [grads_out, *near, along_y(far, HOPS[3])]
     terms = scatter_rest(total)

time: 161 us -> 165 us (1.025)
  blocking collectives: 84.3 us -> 35.7 us
  waiting for transfers between devices: 10.4 us -> 55.7 us
  starting transfers between devices: 14 us -> 18 us
  local copies, waits for them, and re-layouts: 5.95 us -> 7.85 us
    all_to_all x1 -> x0, blocking collectives: 48.6 us -> none  [scatter_group(): return jnp.sum(lax.all_to_all(both, GROUP, 0, 0, tiled=True), axis=0)]
    ppermute x6 -> x9, waiting for transfers between devices: 7.63 us -> 52.9 us  [along_y(): lax.ppermute(value, ('ylo', 'yhi'), [(place_of(i), place_of((i + hop) % 4...]
    ppermute x6 -> x9, starting transfers between devices: 8.04 us -> 11.9 us  [along_y(): lax.ppermute(value, ('ylo', 'yhi'), [(place_of(i), place_of((i + hop) % 4...]
    add x0 -> x2, other arithmetic: none -> 2.12 us  [the longest x1 1.1 us: scatter_group(): mine = mine + lax.ppermute(other, 'core', [(0, 1), (1, 0)])]
  transfers between devices with their start and end apart: 9 -> 13, of which waited for: 3 -> 5; matrix products, arithmetic and copies ran while one was open for 8% -> 9% of each run, Pallas kernels for 13% -> 12%
where the time goes in v6:
time: 165 us; the launch traced here: 164 us
  waiting for transfers between devices  55.7 us (34%)
  blocking collectives  35.7 us (22%)
  Pallas kernels  22.8 us (14%)
  starting transfers between devices  18 us (11%)
  between operations  14.2 us (9%)
  local copies, waits for them, and re-layouts  7.85 us (5%)
  other arithmetic  5.05 us (3%)
  matrix products  4.8 us (3%)
    ppermute x9, waiting for transfers between devices, along_y(): lax.ppermute(value, ('ylo', 'yhi'), [(place_of(i), place_of((i + hop) % 4...  52.9 us
    all_to_all x1, blocking collectives, scatter_rest(): lax.all_to_all(mine.reshape(32, 1, mine.size // 32), REST, 0, 0, tiled=True)  21.1 us
    pallas_call x2, Pallas kernels, product(): pl.pallas_call(functools.partial(product_kernel, n), out_shape=[jax.Shape...  20.2 us
    all_to_all x1, blocking collectives, gather_by_exchange(): lax.all_to_all(jnp.broadcast_to(value[None], (n, *value.shape)), axes, 0,...  14.6 us
    ppermute x9, starting transfers between devices, along_y(): lax.ppermute(value, ('ylo', 'yhi'), [(place_of(i), place_of((i + hop) % 4...  11.9 us
    all_to_all x1, starting transfers between devices, gather_by_exchange(): lax.all_to_all(jnp.broadcast_to(value[None], (n, *value.shape)), axes, 0,...  4.4 us
  transfers between devices with their start and end apart: 13, of which 5 were waited for; matrix products, arithmetic and copies ran while one was open for 9% of the time, Pallas kernels for 12%

profile of v6, /device:TPU:2, one launch (start us, length us, event | category | flops | bytes accessed | tf_op | source)
XLA Modules:
  0.0 164.1 jit_solution(17923225713378943232)
XLA Ops:
  7.2 1.0 constant_dynamic-slice_fusion.3
  8.2 1.7 %collective-permute-start = (bf16[256,256]{1,0:T(8,128)(2,1)S(1)}, bf16[256,256]{1,0:T(8,128)(2,1)S(1)}, u32[]{:S(2)}, u32[]{:S(2)}) collective-permute-start(bf16[256,256]{1,0:T(8,128)(2,1)S(1)} %constant_dynamic-slice_fusion.3), channel_id=1, source_target_pairs={{0,128},{128,0},{1,129},{129,1},{2,130},{130,2},{3,131},{131,3},{4... | collective-permute-start | bytes 393224 | tf_op jit(solution)/shard_map/ppermute | solution.py:176
  9.9 0.9 dynamic-slice_bitcast_fusion
  10.8 2.7 %collective-permute-done = bf16[256,256]{1,0:T(8,128)(2,1)S(1)} collective-permute-done((bf16[256,256]{1,0:T(8,128)(2,1)S(1)}, bf16[256,256]{1,0:T(8,128)(2,1)S(1)}, u32[]{:S(2)}, u32[]{:S(2)}) %collective-permute-start) | collective-permute-done | bytes 131104 | tf_op jit(solution)/shard_map/ppermute | solution.py:176
  14.4 2.4 %convolution_convert_fusion.refs_4_ = bf16[128,16]{1,0:T(8,128)(2,1)S(1)} fusion(bf16[128,8192]{1,0:T(8,128)(2,1)} %refs_0_.1, bf16[16,8192]{1,0:T(8,128)(2,1)} %param.9), kind=kOutput, calls=%fused_computation.2 | convolution fusion | flops 33556480 | bytes 2363392 | tf_op jit(solution)/shard_map/td,rd->tr/dot_general | solution.py:182
  17.8 2.1 %convolution_multiply_fusion = f32[16,8192]{1,0:T(8,128)} fusion(bf16[128,8192]{1,0:T(8,128)(2,1)S(1)} %copy-done.1, bf16[128,4096]{1,0:T(8,128)(2,1)S(1)} %copy-done, bf16[16,4096]{1,0:T(8,128)(2,1)S(1)} %copy-done.2), kind=kOutput, calls=%fused_computation | convolution fusion | flops 50464768 | bytes 3801088 | tf_op jit(solution)/shard_map/tr,td->rd/dot_general | solution.py:184
  19.8 1.8 %fusion = f32[16,6144]{1,0:T(8,128)} fusion(s32[]{:T(128)S(6)} %select_n.59, f32[16,8192]{1,0:T(8,128)} %convolution_multiply_fusion, f32[16,4096]{1,0:T(8,128)S(1)} %convolution_multiply_fusion.1), kind=kLoop, calls=%fused_computation.8 | loop fusion | flops 98304 | bytes 1179652 | tf_op jit(solution)/shard_map/concatenate | solution.py:31
  21.7 1.6 collective-permute-start.5
  23.2 1.7 %collective-permute-start.6 = (bf16[128,8192]{1,0:T(8,128)(2,1)S(1)}, bf16[128,8192]{1,0:T(8,128)(2,1)}, u32[]{:S(2)}, u32[]{:S(2)}) collective-permute-start(bf16[128,8192]{1,0:T(8,128)(2,1)S(1)} %copy-done.1), channel_id=1, source_target_pairs={{0,129},{128,0},{1,128},{129,1},{2,131},{130,2},{3,130},{131,3},{4... | collective-permute-start | bytes 6291464 | tf_op jit(solution)/shard_map/ppermute | solution.py:27
  24.9 1.1 fusion.2
  27.8 2.8 %collective-permute-start.3 = (f32[16,1536]{1,0:T(8,128)}, f32[16,1536]{1,0:T(8,128)}, u32[]{:S(2)}, u32[]{:S(2)}) collective-permute-start(f32[16,1536]{1,0:T(8,128)} %get-tuple-element.23), channel_id=1, source_target_pairs={{0,129},{128,0},{1,128},{129,1},{2,131},{130,2},{3,130},{131,3},{4... | collective-permute-start | bytes 294920 | tf_op jit(solution)/shard_map/ppermute | solution.py:27
  31.5 41.6 %collective-permute-done.2 = f32[16,1536]{1,0:T(8,128)S(1)} collective-permute-done((f32[16,1536]{1,0:T(8,128)}, f32[16,1536]{1,0:T(8,128)S(1)}, u32[]{:S(2)}, u32[]{:S(2)}) %collective-permute-start.2) | collective-permute-done | bytes 98336 | tf_op jit(solution)/shard_map/ppermute | solution.py:27
  73.9 2.6 %collective-permute-done.4 = f32[16,1536]{1,0:T(8,128)} collective-permute-done((f32[16,1536]{1,0:T(8,128)S(1)}, f32[16,1536]{1,0:T(8,128)}, u32[]{:S(2)}, u32[]{:S(2)}) %collective-permute-start.4) | collective-permute-done | bytes 98336 | tf_op jit(solution)/shard_map/ppermute | solution.py:27
  76.5 1.0 add_add_fusion
  78.5 21.1 %all_to_all.15 = f32[32,1,768]{2,1,0:T(1,128)S(1)} all-to-all(f32[32,1,768]{2,1,0:T(1,128)S(1)} %reshape.79), channel_id=1, replica_groups=mesh['ylo'=2,'z'=8,'core'=2,'x'=4,'yhi'=2] {'x','z'}, dimensions={0} | all-to-all | bytes 196608 | tf_op jit(solution)/shard_map/all_to_all | solution.py:43
  99.7 14.6 %all_to_all.16 = f32[32,1,768]{2,1,0:T(1,128)S(1)} all-to-all(f32[32,1,768]{2,1,0:T(1,128)S(1)} %broadcast_in_dim.17), channel_id=1, replica_groups=mesh['ylo'=2,'z'=8,'core'=2,'x'=4,'yhi'=2] {'x','z'}, dimensions={0} | all-to-all | bytes 196608 | tf_op jit(solution)/shard_map/all_to_all | solution.py:23
  114.5 1.0 broadcast_in_dim.19
  115.5 4.4 %all-to-all-start.2 = ((f32[8,16,1536]{2,1,0:T(8,128)}), f32[8,16,1536]{2,1,0:T(8,128)}, u32[]{:S(2)}, u32[]{:S(2)}) async-start(f32[8,16,1536]{2,1,0:T(8,128)} %broadcast_in_dim.19), calls=%async_computation.2 | async-start | bytes 1572864 | tf_op jit(solution)/shard_map/all_to_all | solution.py:23
  119.9 7.9 %collective-permute-done.7.refs_0_ = bf16[128,8192]{1,0:T(8,128)(2,1)} collective-permute-done((bf16[128,8192]{1,0:T(8,128)(2,1)S(1)}, bf16[128,8192]{1,0:T(8,128)(2,1)}, u32[]{:S(2)}, u32[]{:S(2)}) %collective-permute-start.7) | collective-permute-done | bytes 2097184 | tf_op jit(solution)/shard_map/ppermute | solution.py:27
  127.8 11.8 %shard_map.77 = (bf16[128,1024]{1,0:T(8,128)(2,1)}, bf16[128,1024]{1,0:T(8,128)(2,1)}, bf16[128,1024]{1,0:T(8,128)(2,1)}) custom-call(bf16[128,8192]{1,0:T(8,128)(2,1)} %collective-permute-done.7.refs_0_, bf16[128,8192]{1,0:T(8,128)(2,1)} %collective-permute-done.5.refs_1_, bf16[128,8192]{1,0:T(8,128)(2,1)} %collective-permute-done.6.refs_2_, ...), custom_call_target="tpu_custom_call" | custom-call | flops 6442450944 | bytes 23855104 | tf_op jit(solution)/shard_map/pallas_call | solution.py:112
  140.5 3.0 %collective-permute-start.8 = (bf16[128,1024]{1,0:T(8,128)(2,1)}, bf16[128,1024]{1,0:T(8,128)(2,1)}, u32[]{:S(2)}, u32[]{:S(2)}) collective-permute-start(bf16[128,1024]{1,0:T(8,128)(2,1)} %get-tuple-element.17), channel_id=1, source_target_pairs={{0,129},{128,0},{1,128},{129,1},{2,131},{130,2},{3,130},{131,3},{4... | collective-permute-start | bytes 786440 | tf_op jit(solution)/shard_map/ppermute | solution.py:27
  143.5 1.2 copy.15
  146.3 8.4 %shard_map.76.refs_0_ = bf16[128,1024]{1,0:T(8,128)(2,1)S(1)} custom-call(bf16[128,8192]{1,0:T(8,128)(2,1)S(1)} %copy-done.1, bf16[4,16,256,512]{3,2,1,0:T(8,128)(2,1)} %bitcast.16), custom_call_target="tpu_custom_call" | custom-call | flops 2147483648 | bytes 19136512 | tf_op jit(solution)/shard_map/pallas_call | solution.py:112
  154.7 2.6 %shard_map.78 = bf16[128,4096]{1,0:T(8,128)(2,1)} custom-call(s32[1]{0:T(128)} %bitcast.place, bf16[128,1024]{1,0:T(8,128)(2,1)S(1)} %shard_map.76.refs_0_, bf16[128,1024]{1,0:T(8,128)(2,1)} %collective-permute-done.8.refs_1_, bf16[128,1024]{1,0:T(8,128)(2,1)} %collective-permute-done.9.refs_2_, bf16[128,1024]{1,0:T(8,128)(2,1)S(1)} %collective-permute-done.10.refs_3_, ...), custom_call_target="tpu_custom_call" | custom-call | flops 16777216 | bytes 2097152 | tf_op jit(solution)/shard_map/pallas_call | solution.py:153
  (39 shorter events, 9.0 us)
Async XLA Ops:
  7.2 9.7 %copy-start = (bf16[128,4096]{1,0:T(8,128)(2,1)S(1)}, bf16[128,4096]{1,0:T(8,128)(2,1)}, u32[]{:S(2)}) copy-start(bf16[128,4096]{1,0:T(8,128)(2,1)} %param.5) | copy-start | bytes 3145732
  7.2 120.7 %all-gather.2.cloned.1.call-start = ((), (), s32[]{:S(2)}) async-start(), calls=%async_computation.3 | async-start | bytes 17039360 | tf_op jit(solution)/shard_map/all_gather | solution.py:178
  8.2 5.3 %collective-permute-start = (bf16[256,256]{1,0:T(8,128)(2,1)S(1)}, bf16[256,256]{1,0:T(8,128)(2,1)S(1)}, u32[]{:S(2)}, u32[]{:S(2)}) collective-permute-start(bf16[256,256]{1,0:T(8,128)(2,1)S(1)} %constant_dynamic-slice_fusion.3), channel_id=1, source_target_pairs={{0,128},{128,0},{1,129},{129,1},{2,130},{130,2},{3,131},{131,3},{4... | collective-permute-start | bytes 393224 | tf_op jit(solution)/shard_map/ppermute | solution.py:176
  14.4 3.4 %copy-start.1 = (bf16[128,8192]{1,0:T(8,128)(2,1)S(1)}, bf16[128,8192]{1,0:T(8,128)(2,1)}, u32[]{:S(2)}) copy-start(bf16[128,8192]{1,0:T(8,128)(2,1)} %refs_0_.1) | copy-start | bytes 6291460
  14.4 3.4 %copy-start.2 = (bf16[16,4096]{1,0:T(8,128)(2,1)S(1)}, bf16[16,4096]{1,0:T(8,128)(2,1)}, u32[]{:S(2)}) copy-start(bf16[16,4096]{1,0:T(8,128)(2,1)} %refs_5_.1) | copy-start | bytes 393220
  17.1 0.6 copy-start.3
  21.6 3.2 %collective-permute-start.1 = (f32[16,6144]{1,0:T(8,128)}, f32[16,6144]{1,0:T(8,128)}, u32[]{:S(2)}, u32[]{:S(2)}) collective-permute-start(f32[16,6144]{1,0:T(8,128)} %fusion), channel_id=1, source_target_pairs={{0,8},{8,0},{1,9},{9,1},{2,10},{10,2},{3,11},{11,3},{4,12},{12,4},... | collective-permute-start | bytes 1179656 | tf_op jit(solution)/shard_map/ppermute | solution.py:35
  21.7 55.8 %collective-permute-start.5 = (bf16[128,8192]{1,0:T(8,128)(2,1)S(1)}, bf16[128,8192]{1,0:T(8,128)(2,1)}, u32[]{:S(2)}, u32[]{:S(2)}) collective-permute-start(bf16[128,8192]{1,0:T(8,128)(2,1)S(1)} %copy-done.1), channel_id=1, source_target_pairs={{0,128},{128,1},{1,129},{129,0},{2,130},{130,3},{3,131},{131,2},{4... | collective-permute-start | bytes 6291464 | tf_op jit(solution)/shard_map/ppermute | solution.py:27
  23.2 54.3 %collective-permute-start.6 = (bf16[128,8192]{1,0:T(8,128)(2,1)S(1)}, bf16[128,8192]{1,0:T(8,128)(2,1)}, u32[]{:S(2)}, u32[]{:S(2)}) collective-permute-start(bf16[128,8192]{1,0:T(8,128)(2,1)S(1)} %copy-done.1), channel_id=1, source_target_pairs={{0,129},{128,0},{1,128},{129,1},{2,131},{130,2},{3,130},{131,3},{4... | collective-permute-start | bytes 6291464 | tf_op jit(solution)/shard_map/ppermute | solution.py:27
  26.0 0.7 copy-start.5
  27.4 45.6 %collective-permute-start.2 = (f32[16,1536]{1,0:T(8,128)}, f32[16,1536]{1,0:T(8,128)S(1)}, u32[]{:S(2)}, u32[]{:S(2)}) collective-permute-start(f32[16,1536]{1,0:T(8,128)} %get-tuple-element.21), channel_id=1, source_target_pairs={{0,128},{128,1},{1,129},{129,0},{2,130},{130,3},{3,131},{131,2},{4... | collective-permute-start | bytes 294920 | tf_op jit(solution)/shard_map/ppermute | solution.py:27
  27.8 46.1 %collective-permute-start.3 = (f32[16,1536]{1,0:T(8,128)}, f32[16,1536]{1,0:T(8,128)}, u32[]{:S(2)}, u32[]{:S(2)}) collective-permute-start(f32[16,1536]{1,0:T(8,128)} %get-tuple-element.23), channel_id=1, source_target_pairs={{0,129},{128,0},{1,128},{129,1},{2,131},{130,2},{3,130},{131,3},{4... | collective-permute-start | bytes 294920 | tf_op jit(solution)/shard_map/ppermute | solution.py:27
  30.7 45.8 %collective-permute-start.4 = (f32[16,1536]{1,0:T(8,128)S(1)}, f32[16,1536]{1,0:T(8,128)}, u32[]{:S(2)}, u32[]{:S(2)}) collective-permute-start(f32[16,1536]{1,0:T(8,128)S(1)} %get-tuple-element.22), channel_id=1, source_target_pairs={{0,1},{128,129},{1,0},{129,128},{2,3},{130,131},{3,2},{131,130},{4... | collective-permute-start | bytes 294920 | tf_op jit(solution)/shard_map/ppermute | solution.py:27
  77.5 50.3 %collective-permute-start.7 = (bf16[128,8192]{1,0:T(8,128)(2,1)S(1)}, bf16[128,8192]{1,0:T(8,128)(2,1)}, u32[]{:S(2)}, u32[]{:S(2)}) collective-permute-start(bf16[128,8192]{1,0:T(8,128)(2,1)S(1)} %copy-done.1), channel_id=1, source_target_pairs={{0,1},{128,129},{1,0},{129,128},{2,3},{130,131},{3,2},{131,130},{4... | collective-permute-start | bytes 6291464 | tf_op jit(solution)/shard_map/ppermute | solution.py:27
  115.5 28.0 %all-to-all-start.2 = ((f32[8,16,1536]{2,1,0:T(8,128)}), f32[8,16,1536]{2,1,0:T(8,128)}, u32[]{:S(2)}, u32[]{:S(2)}) async-start(f32[8,16,1536]{2,1,0:T(8,128)} %broadcast_in_dim.19), calls=%async_computation.2 | async-start | bytes 1572864 | tf_op jit(solution)/shard_map/all_to_all | solution.py:23
  139.7 14.9 %collective-permute-start.10 = (bf16[128,1024]{1,0:T(8,128)(2,1)}, bf16[128,1024]{1,0:T(8,128)(2,1)S(1)}, u32[]{:S(2)}, u32[]{:S(2)}) collective-permute-start(bf16[128,1024]{1,0:T(8,128)(2,1)} %get-tuple-element.19), channel_id=1, source_target_pairs={{0,1},{128,129},{1,0},{129,128},{2,3},{130,131},{3,2},{131,130},{4... | collective-permute-start | bytes 786440 | tf_op jit(solution)/shard_map/ppermute | solution.py:27
  140.5 14.1 %collective-permute-start.8 = (bf16[128,1024]{1,0:T(8,128)(2,1)}, bf16[128,1024]{1,0:T(8,128)(2,1)}, u32[]{:S(2)}, u32[]{:S(2)}) collective-permute-start(bf16[128,1024]{1,0:T(8,128)(2,1)} %get-tuple-element.17), channel_id=1, source_target_pairs={{0,129},{128,0},{1,128},{129,1},{2,131},{130,2},{3,130},{131,3},{4... | collective-permute-start | bytes 786440 | tf_op jit(solution)/shard_map/ppermute | solution.py:27
  143.5 11.1 %collective-permute-start.9 = (bf16[128,1024]{1,0:T(8,128)(2,1)}, bf16[128,1024]{1,0:T(8,128)(2,1)}, u32[]{:S(2)}, u32[]{:S(2)}) collective-permute-start(bf16[128,1024]{1,0:T(8,128)(2,1)} %get-tuple-element.18), channel_id=1, source_target_pairs={{0,128},{128,1},{1,129},{129,0},{2,130},{130,3},{3,131},{131,2},{4... | collective-permute-start | bytes 786440 | tf_op jit(solution)/shard_map/ppermute | solution.py:27
  146.3 8.4 %copy-start.4 = (bf16[128,16]{1,0:T(8,128)(2,1)S(1)}, bf16[128,16]{1,0:T(8,128)(2,1)}, u32[]{:S(2)}) copy-start(bf16[128,16]{1,0:T(8,128)(2,1)} %copy-done.3) | copy-start | bytes 12292
Sparse Core Ops, SparseCore 0:
  14.5 105.5 all-gather.1
